TPU v7x, 32 devices: a whole 2x2x4 slice. The times are simulated.
32 devices in a mesh: grp: 4 (over y, x), fac: 8 (over z, core).
Axes of the slice: x: 2, y: 2, z: 4, core: 2. Of those that a mesh axis runs over, the one named last changes fastest.
Arguments:
- image_cube: float32 [32, 1536, 256], P('fac', 'grp'), may hold values from -6 to 6
- dual: bfloat16 [8, 32, 2304, 256], P(None, None, ('grp', 'fac')), may hold values from -6 to 6
- lowpass: bfloat16 [2, 4], replicated, may hold values from -2.5 to 2.5, as said below
- thresholds: float32 [8], replicated, may hold values from 4 to 16
- facet_rows: int32 [4, 8], replicated, may hold values from 24 to 72, as said below
Outputs:
- dual_next: bfloat16 [8, 32, 2304, 256], P(None, None, ('grp', 'fac'))
- prior_term: float32 [32, 1536, 256], P('fac', 'grp')
Inputs may be any that keep to these rules, and one draw needn't show every extreme that they name: `facet_rows`: every row sums to 384; in every row some facet has exactly 72 rows and some exactly 24. `lowpass`: row d has nonzero taps only at positions 2 - d - 1 to 2 + d.
All inputs are finite; a program needn't handle non-finite values.
Results may differ from a plain program's by a relative error of at most 0.0035.
Values sent between devices are 32-bit elements; how exact they have to be, the bound alone decides.
A program may use at most 128 MiB of HBM per device.

v0:
```python
import jax
import jax.numpy as jnp
from jax import lax
from jax.sharding import PartitionSpec as P


def shifted(x, axis, by):
    devices = lax.axis_size(axis)
    pairs = [(i, i + by) for i in range(devices) if 0 <= i + by < devices]
    return lax.ppermute(x, axis, pairs)


def highpass(lowpass_row):
    tap_count = lowpass_row.shape[0]
    parity = jnp.where(jnp.arange(tap_count) % 2 == 0, 1.0, -1.0).astype(jnp.float32)
    return parity * lowpass_row[::-1]


def column_filter(source, filter_taps):
    halo_rows = filter_taps.shape[0] // 2
    length = source.shape[2]
    padded = jnp.pad(source, ((0, 0), (0, 0), (halo_rows, halo_rows)))
    summed = jnp.zeros_like(source)
    for offset in range(2 * halo_rows):
        summed = summed + filter_taps[offset] * lax.slice_in_dim(
            padded, offset, offset + length, axis=2
        )
    return summed


def column_adjoint(source, filter_taps):
    halo_rows = filter_taps.shape[0] // 2
    length = source.shape[2]
    padded = jnp.pad(source, ((0, 0), (0, 0), (halo_rows, halo_rows)))
    summed = jnp.zeros_like(source)
    for offset in range(2 * halo_rows):
        begin = 2 * halo_rows - offset
        summed = summed + filter_taps[offset] * lax.slice_in_dim(
            padded, begin, begin + length, axis=2
        )
    return summed


def row_filter(extended, filter_taps, capacity):
    summed = jnp.zeros((extended.shape[0], capacity, extended.shape[2]), jnp.float32)
    for offset in range(filter_taps.shape[0]):
        summed = summed + filter_taps[offset] * lax.slice_in_dim(
            extended, offset, offset + capacity, axis=1
        )
    return summed


def row_adjoint(scaled_wide, filter_taps, extended_rows):
    capacity = scaled_wide.shape[1]
    spare = extended_rows - capacity
    summed = jnp.zeros((scaled_wide.shape[0], extended_rows, scaled_wide.shape[2]), jnp.float32)
    for offset in range(filter_taps.shape[0]):
        summed = summed + filter_taps[offset] * jnp.pad(
            scaled_wide, ((0, 0), (offset, spare - offset), (0, 0))
        )
    return summed


def on_device(image_cube, dual, lowpass, thresholds, facet_rows):
    filters_wide = lowpass.astype(jnp.float32)
    groups = lax.axis_size("fac")
    band_index = lax.axis_index("grp")
    facet_index = lax.axis_index("fac")
    local_channels, band_rows, columns = image_cube.shape
    capacity = dual.shape[2]
    halo_rows = lowpass.shape[1] // 2
    extended_rows = capacity + 2 * halo_rows
    band_lengths = lax.dynamic_index_in_dim(facet_rows, band_index, 0, keepdims=False)
    band_starts = jnp.cumsum(band_lengths) - band_lengths
    own_length = band_lengths[facet_index]
    positions = jnp.arange(capacity)
    row_index = band_starts[:, None] + positions[None, :]
    keep_mask = positions[None, :] < band_lengths[:, None]
    picked = jnp.take(image_cube, jnp.clip(row_index, 0, band_rows - 1), axis=1)
    picked = jnp.where(keep_mask[None, :, :, None], picked, 0.0)
    received = lax.all_to_all(picked, "fac", split_axis=1, concat_axis=0, tiled=True)
    own_rows = received.reshape(-1, capacity, columns)
    last_rows = lax.dynamic_slice_in_dim(own_rows, own_length - halo_rows, halo_rows, 1)
    upper_rim = shifted(last_rows, ("grp", "fac"), 1)
    lower_rim = shifted(own_rows[:, :halo_rows], ("grp", "fac"), -1)
    extended = jnp.concatenate([upper_rim, own_rows, jnp.zeros_like(upper_rim)], axis=1)
    extended = lax.dynamic_update_slice_in_dim(extended, lower_rim, halo_rows + own_length, 1)
    channels = extended.shape[0]
    valid_rows = (positions < own_length).astype(jnp.float32)[None, :, None]
    merged = jnp.zeros((channels, extended_rows, columns), jnp.float32)
    updated = []
    for dict_index in range(lowpass.shape[0]):
        low_taps = filters_wide[dict_index]
        filter_pair = (low_taps, highpass(low_taps))
        filtered = [column_filter(extended, taps_one) for taps_one in filter_pair]
        row_sums = [
            jnp.zeros((channels, extended_rows, columns), jnp.float32),
            jnp.zeros((channels, extended_rows, columns), jnp.float32),
        ]
        for row_kind in range(2):
            for column_kind in range(2):
                subband = 4 * dict_index + 2 * row_kind + column_kind
                coefficient = row_filter(filtered[column_kind], filter_pair[row_kind], capacity)
                combined = (dual[subband].astype(jnp.float32) + coefficient) * valid_rows
                magnitude = jnp.sqrt(jnp.sum(combined * combined, axis=0))
                radius = thresholds[subband]
                scaled = (combined * (radius / jnp.maximum(magnitude, radius))).astype(jnp.bfloat16)
                updated.append(scaled)
                row_sums[column_kind] = row_sums[column_kind] + row_adjoint(
                    scaled.astype(jnp.float32), filter_pair[row_kind], extended_rows
                )
        for column_kind in range(2):
            merged = merged + column_adjoint(row_sums[column_kind], filter_pair[column_kind])
    own_part = merged[:, halo_rows : halo_rows + capacity] * valid_rows
    spill_down = lax.dynamic_slice_in_dim(merged, halo_rows + own_length, halo_rows, 1)
    from_previous = shifted(spill_down, ("grp", "fac"), 1)
    from_next = shifted(merged[:, :halo_rows], ("grp", "fac"), -1)
    own_part = own_part.at[:, :halo_rows].add(from_previous)
    closing = lax.dynamic_slice_in_dim(own_part, own_length - halo_rows, halo_rows, 1) + from_next
    own_part = lax.dynamic_update_slice_in_dim(own_part, closing, own_length - halo_rows, 1)
    returned = lax.all_to_all(own_part[:, None], "fac", split_axis=0, concat_axis=1, tiled=True)
    band_positions = jnp.arange(band_rows)
    owner_facet = (
        jnp.sum((band_starts[None, :] <= band_positions[:, None]).astype(jnp.int32), axis=1) - 1
    )
    slot_index = owner_facet * capacity + band_positions - band_starts[owner_facet]
    prior_term = jnp.take(
        returned.reshape(local_channels, groups * capacity, columns), slot_index, axis=1
    )
    return (jnp.stack(updated, 0), prior_term)


def solution(mesh):
    placed = (P("fac", "grp", None), P(None, None, ("grp", "fac"), None), P(), P(), P())
    return jax.shard_map(
        on_device,
        mesh=mesh,
        in_specs=placed,
        out_specs=(P(None, None, ("grp", "fac"), None), P("fac", "grp", None)),
        check_vma=False,
    )
```

profile of v0, /device:TPU:4, one launch (start us, length us, event | category | flops | bytes accessed | tf_op | source)
XLA Modules:
  0.0 302.8 jit_solution(14397929988691386308)
XLA Ops:
  3.3 6.5 %gather_fusion = f32[576,4,256]{2,0,1:T(8,128)} fusion(f32[4,384,256]{2,1,0:T(8,128)S(1)} %copy-done, s32[1024]{0:T(1024)S(1)} %pad_clamp_fusion.1), kind=kCustom, calls=%fused_computation | custom fusion | bytes 4720896 | tf_op jit(solution)/shard_map/jit(_take)/gather | solution.py:79
  9.8 3.4 %fusion.36 = f32[4,8,72,256]{3,2,0,1:T(8,128)} fusion(f32[8,72,4,256]{3,1,0,2:T(8,128)} %bitcast.123, pred[8,72]{1,0:T(8,128)(4,1)S(1)} %get-tuple-element.95, pred[8,72]{1,0:T(8,128)(4,1)S(1)} %get-tuple-element.96), kind=kLoop, calls=%fused_computation.72 | loop fusion | flops 1179648 | bytes 4719744 | tf_op jit(solution)/shard_map/jit(_where)/select_n | solution.py:80
  13.2 5.0 %all-to-all-start = ((f32[4,8,72,256]{3,2,0,1:T(8,128)}), f32[4,8,72,256]{3,2,0,1:T(8,128)S(1)}, u32[]{:S(2)}, u32[]{:S(2)}) async-start(f32[4,8,72,256]{3,2,0,1:T(8,128)} %fusion.36), calls=%async_computation | async-start | bytes 4718592 | tf_op jit(solution)/shard_map/all_to_all | solution.py:81
  24.3 48.6 %all-to-all-done = f32[4,8,72,256]{3,2,0,1:T(8,128)S(1)} async-done(((f32[4,8,72,256]{3,2,0,1:T(8,128)}), f32[4,8,72,256]{3,2,0,1:T(8,128)S(1)}, u32[]{:S(2)}, u32[]{:S(2)}) %all-to-all-start) | async-done | bytes 2359328 | tf_op jit(solution)/shard_map/all_to_all | solution.py:81
  75.5 7.4 %collective-permute-start.1 = (f32[32,2,256]{2,1,0:T(2,128)S(1)}, f32[32,2,256]{2,1,0:T(2,128)S(1)}, u32[]{:S(2)}, u32[]{:S(2)}) collective-permute-start(f32[32,2,256]{2,1,0:T(2,128)S(1)} %get-tuple-element.55), channel_id=1, source_target_pairs={{1,0},{2,1},{3,2},{4,3},{5,4},{6,5},{7,6},{8,7},{9,8},{10,9},{11,1... | collective-permute-start | bytes 196616 | tf_op jit(solution)/shard_map/ppermute | solution.py:10
  85.5 4.6 %multiply_add_fusion.3 = f32[32,76,256]{2,1,0:T(8,128)S(1)} fusion(f32[32,76,256]{2,1,0:T(8,128)S(1)} %dynamic_update_slice.7, f32[]{:T(128)} %bitcast.15, f32[]{:T(128)} %bitcast.14, f32[]{:T(128)} %bitcast.13, f32[]{:T(128)} %bitcast.1), kind=kLoop, calls=%fused_computation.52 | loop fusion | flops 4358144 | bytes 4980752 | tf_op jit(solution)/shard_map/add | solution.py:25
  90.0 10.0 %multiply_reduce_fusion.5 = (f32[72,256]{1,0:T(8,128)S(1)}, f32[32,72,256]{2,1,0:T(8,128)}, f32[72,256]{1,0:T(8,128)S(1)}, f32[32,72,256]{2,1,0:T(8,128)}) fusion(f32[72]{0:T(128)S(1)} %compare_convert_fusion, f32[32,76,256]{2,1,0:T(8,128)S(1)} %multiply_add_fusion.3, f32[]{:T(128)} %bitcast.23, f32[]{:T(128)} %bitcast.22, f32[]{:T(128)} %bitcast.21, ...), kind=kLoop, calls=%fused_computation.84 | loop fusion | flops 14118912 | bytes 16662848 | tf_op jit(solution)/shard_map/reduce_sum | solution.py:105
  100.0 13.5 %multiply_add_fusion = (f32[32,76,256]{2,1,0:T(8,128)S(1)}, f32[32,76,256]{2,1,0:T(8,128)S(1)}, f32[32,76,256]{2,1,0:T(8,128)S(1)}) fusion(f32[32,76,256]{2,1,0:T(8,128)S(1)} %dynamic_update_slice.7, f32[]{:T(128)} %bitcast.44, f32[]{:T(128)} %bitcast.43, f32[]{:T(128)} %bitcast.42, f32[]{:T(128)} %bitcast.41, f32[]{:T(128)} %bitcast.36, f32[]{:T(128)} %bitcast.35, ...), kind=kLoop, calls=%fused_computation.49 | loop fusion | flops 13074432 | bytes 9961520 | tf_op jit(solution)/shard_map/add | solution.py:25
  113.5 8.3 %multiply_reduce_fusion = (f32[72,256]{1,0:T(8,128)S(1)}, f32[32,72,256]{2,1,0:T(8,128)S(1)}, f32[72,256]{1,0:T(8,128)S(1)}, f32[32,72,256]{2,1,0:T(8,128)S(1)}) fusion(f32[72]{0:T(128)S(1)} %compare_convert_fusion, f32[32,76,256]{2,1,0:T(8,128)S(1)} %get-tuple-element.52, f32[]{:T(128)} %bitcast.44, f32[]{:T(128)} %bitcast.43, f32[]{:T(128)} %bitcast.42, ...), kind=kLoop, calls=%fused_computation.74 | loop fusion | flops 14118912 | bytes 16662848 | tf_op jit(solution)/shard_map/reduce_sum | solution.py:105
  121.9 8.4 %multiply_reduce_fusion.1 = (f32[72,256]{1,0:T(8,128)S(1)}, f32[32,72,256]{2,1,0:T(8,128)S(1)}, f32[72,256]{1,0:T(8,128)S(1)}, f32[32,72,256]{2,1,0:T(8,128)S(1)}) fusion(f32[72]{0:T(128)S(1)} %compare_convert_fusion, f32[32,76,256]{2,1,0:T(8,128)S(1)} %get-tuple-element.53, f32[]{:T(128)} %bitcast.44, f32[]{:T(128)} %bitcast.43, f32[]{:T(128)} %bitcast.42, ...), kind=kLoop, calls=%fused_computation.76 | loop fusion | flops 14118912 | bytes 16662848 | tf_op jit(solution)/shard_map/reduce_sum | solution.py:105
  130.3 10.3 %multiply_reduce_fusion.4 = (f32[72,256]{1,0:T(8,128)S(1)}, f32[32,72,256]{2,1,0:T(8,128)S(1)}, f32[72,256]{1,0:T(8,128)S(1)}, f32[32,72,256]{2,1,0:T(8,128)S(1)}) fusion(f32[72]{0:T(128)S(1)} %compare_convert_fusion, f32[32,76,256]{2,1,0:T(8,128)S(1)} %get-tuple-element.54, f32[]{:T(128)} %bitcast.23, f32[]{:T(128)} %bitcast.22, f32[]{:T(128)} %bitcast.21, ...), kind=kLoop, calls=%fused_computation.82 | loop fusion | flops 14118912 | bytes 16662848 | tf_op jit(solution)/shard_map/reduce_sum | solution.py:105
  141.4 2.2 maximum_divide_fusion.7
  144.1 8.6 %add_add_fusion.3 = f32[32,76,256]{2,1,0:T(8,128)} fusion(f32[32,72,256]{2,1,0:T(8,128)S(1)} %fusion.39, f32[32,72,256]{2,1,0:T(8,128)S(1)} %fusion.37, f32[]{:T(128)} %bitcast.23, f32[]{:T(128)} %bitcast.22, f32[]{:T(128)} %bitcast.21, f32[]{:T(128)} %bitcast.20, f32[]{:T(128)} %bitcast.15, f32[]{:T(128)} %bitcast.14, f32[]{:T(128)} %bitcast.13, f32[]{:T(128)} %bitcast.1), kind=kLoop, calls=%fused_computation.48 | loop fusion | flops 9338880 | bytes 7208992 | tf_op jit(solution)/shard_map/add | solution.py:109
  154.5 8.2 %add_add_fusion = f32[32,76,256]{2,1,0:T(8,128)} fusion(f32[32,72,256]{2,1,0:T(8,128)S(1)} %fusion.44, f32[32,72,256]{2,1,0:T(8,128)S(1)} %fusion.42, f32[]{:T(128)} %bitcast.44, f32[]{:T(128)} %bitcast.43, f32[]{:T(128)} %bitcast.42, f32[]{:T(128)} %bitcast.41, f32[]{:T(128)} %bitcast.36, f32[]{:T(128)} %bitcast.35, f32[]{:T(128)} %bitcast.34, f32[]{:T(128)} %bitcast.33), kind=kLoop, calls=%fused_computation.45 | loop fusion | flops 9338880 | bytes 7208992 | tf_op jit(solution)/shard_map/add | solution.py:109
  165.7 8.4 %add_add_fusion.2 = f32[32,76,256]{2,1,0:T(8,128)} fusion(f32[32,72,256]{2,1,0:T(8,128)S(1)} %fusion.40, f32[32,72,256]{2,1,0:T(8,128)S(1)} %fusion.38, f32[]{:T(128)} %bitcast.23, f32[]{:T(128)} %bitcast.22, f32[]{:T(128)} %bitcast.21, f32[]{:T(128)} %bitcast.20, f32[]{:T(128)} %bitcast.15, f32[]{:T(128)} %bitcast.14, f32[]{:T(128)} %bitcast.13, f32[]{:T(128)} %bitcast.1), kind=kLoop, calls=%fused_computation.47 | loop fusion | flops 9338880 | bytes 7208992 | tf_op jit(solution)/shard_map/add | solution.py:109
  174.5 8.2 %add_add_fusion.1 = f32[32,76,256]{2,1,0:T(8,128)} fusion(f32[32,72,256]{2,1,0:T(8,128)S(1)} %fusion.43, f32[32,72,256]{2,1,0:T(8,128)S(1)} %fusion.41, f32[]{:T(128)} %bitcast.44, f32[]{:T(128)} %bitcast.43, f32[]{:T(128)} %bitcast.42, f32[]{:T(128)} %bitcast.41, f32[]{:T(128)} %bitcast.36, f32[]{:T(128)} %bitcast.35, f32[]{:T(128)} %bitcast.34, f32[]{:T(128)} %bitcast.33), kind=kLoop, calls=%fused_computation.46 | loop fusion | flops 9338880 | bytes 7208992 | tf_op jit(solution)/shard_map/add | solution.py:109
  182.6 34.3 %fusion.6 = f32[32,76,256]{2,1,0:T(8,128)} fusion(f32[32,76,256]{2,1,0:T(8,128)} %add_add_fusion.3, f32[32,76,256]{2,1,0:T(8,128)} %add_add_fusion.2, f32[32,76,256]{2,1,0:T(8,128)} %add_add_fusion.1, f32[32,76,256]{2,1,0:T(8,128)} %add_add_fusion, f32[]{:T(128)} %bitcast.44, f32[]{:T(128)} %bitcast.43, f32[]{:T(128)} %bitcast.42, f32[]{:T(128)} %bitcast.41, ...), kind=kLoop, calls=%fused_computation.23 | loop fusion | flops 19300352 | bytes 12451904 | tf_op jit(solution)/shard_map/add | solution.py:113
  222.1 7.2 %collective-permute-start.3 = (f32[32,2,256]{2,1,0:T(2,128)S(1)}, f32[32,2,256]{2,1,0:T(2,128)S(1)}, u32[]{:S(2)}, u32[]{:S(2)}) collective-permute-start(f32[32,2,256]{2,1,0:T(2,128)S(1)} %get-tuple-element.50), channel_id=1, source_target_pairs={{1,0},{2,1},{3,2},{4,3},{5,4},{6,5},{7,6},{8,7},{9,8},{10,9},{11,1... | collective-permute-start | bytes 196616 | tf_op jit(solution)/shard_map/ppermute | solution.py:10
  233.2 4.6 %all-to-all-start.1 = ((f32[32,1,72,256]{3,2,1,0:T(8,128)}), f32[32,1,72,256]{3,2,1,0:T(8,128)}, u32[]{:S(2)}, u32[]{:S(2)}) async-start(f32[32,1,72,256]{3,2,1,0:T(8,128)} %dynamic_update_slice.8), calls=%async_computation.1 | async-start | bytes 4718592 | tf_op jit(solution)/shard_map/all_to_all | solution.py:121
  238.6 4.5 %fusion.49 = (s32[384]{0:T(512)S(1)}, s32[384,1]{0,1:T(1,128)S(1)}) fusion(s32[]{:T(128)} %bitcast.56, s32[]{:T(128)} %bitcast.57, s32[]{:T(128)} %bitcast.58, s32[]{:T(128)} %bitcast.59, s32[]{:T(128)} %bitcast.60, s32[]{:T(128)} %bitcast.62, s32[]{:T(128)} %bitcast.61, s32[384]{0:T(512)S(1)} %get-tuple-element.58, s32[384]{0:T(512)S(1)} %get-tuple-element.57), kind=kLoop, calls=%fused_computation.141 | loop fusion | flops 5376 | bytes 6172 | tf_op jit(solution)/shard_map/gather | solution.py:126
  243.9 2.9 bitcast_dynamic-update-slice_fusion.7
  259.6 32.6 %all-to-all-done.1 = f32[32,1,72,256]{3,2,1,0:T(8,128)} async-done(((f32[32,1,72,256]{3,2,1,0:T(8,128)}), f32[32,1,72,256]{3,2,1,0:T(8,128)}, u32[]{:S(2)}, u32[]{:S(2)}) %all-to-all-start.1) | async-done | bytes 2359328 | tf_op jit(solution)/shard_map/all_to_all | solution.py:121
  295.6 3.1 %gather_fusion.1 = f32[384,4,256]{2,1,0:T(4,128)} fusion(f32[4,576,256]{2,0,1:T(4,128)S(1)} %copy.23, s32[1024]{0:T(1024)S(1)} %pad_clamp_fusion), kind=kCustom, calls=%fused_computation.1 | custom fusion | bytes 3147264 | tf_op jit(solution)/shard_map/jit(_take)/gather | solution.py:127
  298.8 2.5 select_bitcast_fusion
  (108 shorter events, 45.7 us)
Async XLA Ops:
  0.6 2.6 copy-start
  13.2 5.0 %copy-start.19 = (s32[4,8]{1,0:T(4,128)S(1)}, s32[4,8]{1,0:T(4,128)}, u32[]{:S(2)}) copy-start(s32[4,8]{1,0:T(4,128)} %param.11) | copy-start | bytes 388
  13.2 8.2 %copy-start.17 = (bf16[2,4]{1,0:T(2,128)(2,1)S(1)}, bf16[2,4]{1,0:T(2,128)(2,1)}, u32[]{:S(2)}) copy-start(bf16[2,4]{1,0:T(2,128)(2,1)} %param.9) | copy-start | bytes 52
  13.2 10.5 %copy-start.18 = (f32[8]{0:T(128)S(1)}, f32[8]{0:T(128)}, u32[]{:S(2)}) copy-start(f32[8]{0:T(128)} %param.10) | copy-start | bytes 100
  13.2 59.7 %all-to-all-start = ((f32[4,8,72,256]{3,2,0,1:T(8,128)}), f32[4,8,72,256]{3,2,0,1:T(8,128)S(1)}, u32[]{:S(2)}, u32[]{:S(2)}) async-start(f32[4,8,72,256]{3,2,0,1:T(8,128)} %fusion.36), calls=%async_computation | async-start | bytes 4718592 | tf_op jit(solution)/shard_map/all_to_all | solution.py:81
  72.9 10.1 %copy-start.16 = (f32[4,8,72,256]{3,2,0,1:T(8,128)}, f32[4,8,72,256]{3,2,0,1:T(8,128)S(1)}, u32[]{:S(2)}) copy-start(f32[4,8,72,256]{3,2,0,1:T(8,128)S(1)} %all-to-all-done) | copy-start | bytes 7077892
  73.0 10.0 %collective-permute-start = (f32[32,2,256]{2,1,0:T(2,128)S(1)}, f32[32,2,256]{2,1,0:T(2,128)S(1)}, u32[]{:S(2)}, u32[]{:S(2)}) collective-permute-start(f32[32,2,256]{2,1,0:T(2,128)S(1)} %get-tuple-element.56), channel_id=1, source_target_pairs={{0,1},{1,2},{2,3},{3,4},{4,5},{5,6},{6,7},{7,8},{8,9},{9,10},{10,1... | collective-permute-start | bytes 196616 | tf_op jit(solution)/shard_map/ppermute | solution.py:10
  75.5 9.6 %collective-permute-start.1 = (f32[32,2,256]{2,1,0:T(2,128)S(1)}, f32[32,2,256]{2,1,0:T(2,128)S(1)}, u32[]{:S(2)}, u32[]{:S(2)}) collective-permute-start(f32[32,2,256]{2,1,0:T(2,128)S(1)} %get-tuple-element.55), channel_id=1, source_target_pairs={{1,0},{2,1},{3,2},{4,3},{5,4},{6,5},{7,6},{8,7},{9,8},{10,9},{11,1... | collective-permute-start | bytes 196616 | tf_op jit(solution)/shard_map/ppermute | solution.py:10
  121.9 32.3 %copy-start.4 = (f32[32,72,256]{2,1,0:T(8,128)}, f32[32,72,256]{2,1,0:T(8,128)S(1)}, u32[]{:S(2)}) copy-start(f32[32,72,256]{2,1,0:T(8,128)S(1)} %get-tuple-element.43) | copy-start | bytes 7077892
  130.2 43.9 %copy-start.9 = (f32[32,72,256]{2,1,0:T(8,128)}, f32[32,72,256]{2,1,0:T(8,128)S(1)}, u32[]{:S(2)}) copy-start(f32[32,72,256]{2,1,0:T(8,128)S(1)} %get-tuple-element.45) | copy-start | bytes 7077892
  130.2 44.1 %copy-start.6 = (f32[32,72,256]{2,1,0:T(8,128)}, f32[32,72,256]{2,1,0:T(8,128)S(1)}, u32[]{:S(2)}) copy-start(f32[32,72,256]{2,1,0:T(8,128)S(1)} %get-tuple-element.29) | copy-start | bytes 7077892
  130.2 13.4 %copy-start.8 = (f32[32,72,256]{2,1,0:T(8,128)S(1)}, f32[32,72,256]{2,1,0:T(8,128)}, u32[]{:S(2)}) copy-start(f32[32,72,256]{2,1,0:T(8,128)} %get-tuple-element.49) | copy-start | bytes 7077892
  140.6 24.8 %copy-start.13 = (f32[32,72,256]{2,1,0:T(8,128)}, f32[32,72,256]{2,1,0:T(8,128)S(1)}, u32[]{:S(2)}) copy-start(f32[32,72,256]{2,1,0:T(8,128)S(1)} %get-tuple-element.47) | copy-start | bytes 7077892
  140.6 25.0 %copy-start.11 = (f32[32,72,256]{2,1,0:T(8,128)}, f32[32,72,256]{2,1,0:T(8,128)S(1)}, u32[]{:S(2)}) copy-start(f32[32,72,256]{2,1,0:T(8,128)S(1)} %get-tuple-element.35) | copy-start | bytes 7077892
  140.6 3.4 %copy-start.2 = (f32[32,72,256]{2,1,0:T(8,128)S(1)}, f32[32,72,256]{2,1,0:T(8,128)}, u32[]{:S(2)}) copy-start(f32[32,72,256]{2,1,0:T(8,128)} %get-tuple-element.37) | copy-start | bytes 7077892
  218.1 11.3 %collective-permute-start.2 = (f32[32,2,256]{2,1,0:T(2,128)S(1)}, f32[32,2,256]{2,1,0:T(2,128)S(1)}, u32[]{:S(2)}, u32[]{:S(2)}) collective-permute-start(f32[32,2,256]{2,1,0:T(2,128)S(1)} %get-tuple-element.51), channel_id=1, source_target_pairs={{0,1},{1,2},{2,3},{3,4},{4,5},{5,6},{6,7},{7,8},{8,9},{9,10},{10,1... | collective-permute-start | bytes 196616 | tf_op jit(solution)/shard_map/ppermute | solution.py:10
  222.1 9.1 %collective-permute-start.3 = (f32[32,2,256]{2,1,0:T(2,128)S(1)}, f32[32,2,256]{2,1,0:T(2,128)S(1)}, u32[]{:S(2)}, u32[]{:S(2)}) collective-permute-start(f32[32,2,256]{2,1,0:T(2,128)S(1)} %get-tuple-element.50), channel_id=1, source_target_pairs={{1,0},{2,1},{3,2},{4,3},{5,4},{6,5},{7,6},{8,7},{9,8},{10,9},{11,1... | collective-permute-start | bytes 196616 | tf_op jit(solution)/shard_map/ppermute | solution.py:10
  233.2 59.1 %all-to-all-start.1 = ((f32[32,1,72,256]{3,2,1,0:T(8,128)}), f32[32,1,72,256]{3,2,1,0:T(8,128)}, u32[]{:S(2)}, u32[]{:S(2)}) async-start(f32[32,1,72,256]{3,2,1,0:T(8,128)} %dynamic_update_slice.8), calls=%async_computation.1 | async-start | bytes 4718592 | tf_op jit(solution)/shard_map/all_to_all | solution.py:121
  237.8 8.9 %copy-start.14 = (f32[32,72,256]{2,1,0:T(8,128)S(1)}, f32[32,72,256]{2,1,0:T(8,128)}, u32[]{:S(2)}) copy-start(f32[32,72,256]{2,1,0:T(8,128)} %copy-done.13) | copy-start | bytes 7077892
  246.7 2.1 copy-start.3
  248.8 2.1 copy-start.12
  250.9 2.1 copy-start.10
  253.0 2.1 copy-start.5
  298.8 4.0 %copy-start.1 = (f32[4,384,256]{2,1,0:T(8,128)S(1)}, f32[4,384,256]{2,1,0:T(8,128)}, u32[]{:S(2)}) copy-start(f32[4,384,256]{2,1,0:T(8,128)} %param.7) | copy-start | bytes 4718596
  (2 other events, 3.9 us)
where the time goes:
time: 306 us; the launch traced here: 303 us
  other arithmetic  160 us (52%)
  waiting for transfers between devices  83 us (27%)
  local copies, waits for them, and re-layouts  28.2 us (9%)
  starting transfers between devices  28.1 us (9%)
  between operations  3.73 us (1%)
    all_to_all x1, waiting for transfers between devices, on_device(): lax.all_to_all(picked, 'fac', split_axis=1, concat_axis=0, tiled=True)  48.6 us
    reduce_sum x4, other arithmetic, on_device(): magnitude = jnp.sqrt(jnp.sum(combined * combined, axis=0))  36.9 us
    add x1, other arithmetic, on_device(): merged + column_adjoint(row_sums[column_kind], filter_pair[column_kind])  34.3 us
    add x4, other arithmetic, on_device(): row_sums[column_kind]  33.4 us
    all_to_all x1, waiting for transfers between devices, on_device(): lax.all_to_all(own_part[:, None], 'fac', split_axis=0, concat_axis=1, til...  32.6 us
    ppermute x4, starting transfers between devices, shifted(): return lax.ppermute(x, axis, pairs)  18.5 us
    add x2, other arithmetic, column_filter(): summed + filter_taps[offset] * lax.slice_in_dim(padded, offset, offset +...  18 us
    unnamed x7, other arithmetic  10.3 us
  transfers between devices with their start and end apart: 6, of which 3 were waited for; matrix products, arithmetic and copies ran while one was open for 9% of the time, Pallas kernels for 0%

commit v1 on v0

v1 whole, which is shorter than its diff:
```python
import functools

import jax
import jax.numpy as jnp
from jax import lax
from jax.experimental import pallas as pl
from jax.experimental.pallas import tpu as pltpu
from jax.sharding import PartitionSpec as P

HALO = 2
LEAD = 8
F32 = jnp.float32
BF16 = jnp.bfloat16


def shifted(x, axis, by):
    devices = lax.axis_size(axis)
    pairs = [(i, i + by) for i in range(devices) if 0 <= i + by < devices]
    return lax.ppermute(x, axis, pairs)


def cut_kernel(cap, starts_ref, image_ref, above_ref, below_ref, out_ref, padded):
    rows = image_ref.shape[1]
    padded[:, 0:LEAD, :] = jnp.zeros_like(padded[:, 0:LEAD, :])
    tail = padded.shape[1] - LEAD - rows
    padded[:, LEAD + rows :, :] = jnp.zeros((padded.shape[0], tail, padded.shape[2]), F32)
    padded[:, LEAD : LEAD + rows, :] = image_ref[...]
    padded[:, LEAD - HALO : LEAD, :] = above_ref[...]
    padded[:, LEAD + rows : LEAD + rows + HALO, :] = below_ref[...]

    @pl.loop(0, out_ref.shape[0])
    def _(pair):
        begin = starts_ref[pair] + (LEAD - HALO)
        base = pl.multiple_of((begin // 8) * 8, 8)
        turn = cap + 8 - (begin - base)

        @pl.loop(0, out_ref.shape[1])
        def _(channel):
            window = padded[channel, pl.ds(base, cap + 8), :]
            out_ref[pair, channel] = pltpu.roll(window, turn, 0)[:cap]


def cut(starts, image, above, below, pairs, cap):
    channels, rows, columns = image.shape
    vmem = pl.BlockSpec(memory_space=pltpu.VMEM)
    return pl.pallas_call(
        functools.partial(cut_kernel, cap),
        out_shape=jax.ShapeDtypeStruct((pairs, channels, cap, columns), F32),
        in_specs=[pl.BlockSpec(memory_space=pltpu.SMEM), vmem, vmem, vmem],
        out_specs=vmem,
        scratch_shapes=[pltpu.VMEM((channels, LEAD + rows + cap + 16, columns), F32)],
        compiler_params=pltpu.CompilerParams(vmem_limit_bytes=48 * 2**20),
    )(starts, image, above, below)


def join_kernel(cap, starts_ref, windows_ref, above_ref, below_ref, out_ref, padded):
    rows = out_ref.shape[1]
    padded[...] = jnp.zeros_like(padded)

    @pl.loop(0, windows_ref.shape[0])
    def _(pair):
        begin = starts_ref[pair] + (LEAD - HALO)
        base = pl.multiple_of((begin // 8) * 8, 8)

        @pl.loop(0, windows_ref.shape[1])
        def _(channel):
            window = windows_ref[pair, channel]
            window = jnp.concatenate([window, jnp.zeros((8, window.shape[1]), F32)], 0)
            here = (channel, pl.ds(base, cap + 8), slice(None))
            padded[here] = padded[here] + pltpu.roll(window, begin - base, 0)

    out_ref[...] = padded[:, LEAD : LEAD + rows, :]
    out_ref[:, 0:HALO, :] = out_ref[:, 0:HALO, :] + above_ref[...]
    out_ref[:, rows - HALO : rows, :] = out_ref[:, rows - HALO : rows, :] + below_ref[...]


def join(starts, windows, above, below, rows):
    pairs, channels, cap, columns = windows.shape
    vmem = pl.BlockSpec(memory_space=pltpu.VMEM)
    return pl.pallas_call(
        functools.partial(join_kernel, cap),
        out_shape=jax.ShapeDtypeStruct((channels, rows, columns), F32),
        in_specs=[pl.BlockSpec(memory_space=pltpu.SMEM), vmem, vmem, vmem],
        out_specs=vmem,
        scratch_shapes=[pltpu.VMEM((channels, LEAD + rows + cap + 16, columns), F32)],
        compiler_params=pltpu.CompilerParams(vmem_limit_bytes=48 * 2**20),
    )(starts, windows, above, below)


GROUP = 8


def prox_kernel(
    facts_ref, taps_ref, thresholds_ref, own_ref, other_ref, ahead_ref, back_ref, dual_ref,
    next_ref, own_out, other_out, image, terms, wide,
):
    step = pl.program_id(0)
    kinds = pl.num_programs(0)
    core, offset, length = facts_ref[0], facts_ref[1], facts_ref[2]
    channels, capacity, columns = dual_ref.shape[1:]
    chips, share, cap, _ = own_ref.shape
    span = capacity + 16
    base = pl.multiple_of(jnp.minimum((offset // 8) * 8, cap - span), 8)
    shift = offset - base
    flat = GROUP * capacity

    @pl.when(step == 0)
    def _():
        for source, half in ((own_ref, core), (other_ref, 1 - core)):
            @pl.loop(0, chips * share)
            def _(i):
                chip, channel = i // share, i % share
                window = source[chip, channel, pl.ds(base, span), :]
                turned = pltpu.roll(window, span - shift, 0)
                image[(2 * chip + half) * share + channel] = turned[: capacity + 8]

    keep = lax.broadcasted_iota(jnp.int32, (capacity, columns), 0) < length

    def analysis(group, sums):
        begin = pl.multiple_of(group * GROUP, GROUP)
        rows = taps_ref[step, 0] * image[pl.ds(begin, GROUP), 0:capacity, :]
        for k in range(1, 2 * HALO):
            rows += taps_ref[step, k] * image[pl.ds(begin, GROUP), k : k + capacity, :]
        rows = rows.reshape(flat, columns)
        high = rows.astype(BF16)
        low = (rows - high.astype(F32)).astype(BF16)
        both = jnp.concatenate([high, low], axis=1)
        coefficient = jnp.dot(both, ahead_ref[0], preferred_element_type=F32)
        out = []
        for b in range(2):
            part = coefficient[:, b * columns : (b + 1) * columns]
            part = part.reshape(GROUP, capacity, columns)
            u = dual_ref[b, pl.ds(begin, GROUP)].astype(F32) + part
            u = jnp.where(keep, u, 0.0)
            wide[b, pl.ds(begin, GROUP)] = u
            out.append(sums[b] + jnp.sum(u * u, axis=0))
        return tuple(out)

    zero = jnp.zeros((capacity, columns), F32)
    sums = lax.fori_loop(0, channels // GROUP, analysis, (zero, zero))
    scales = []
    for b in range(2):
        radius = thresholds_ref[2 * step + b]
        scales.append(radius / jnp.maximum(jnp.sqrt(sums[b]), radius))

    @pl.loop(0, channels // GROUP)
    def _(group):
        begin = pl.multiple_of(group * GROUP, GROUP)
        parts = []
        for b in range(2):
            scaled = (wide[b, pl.ds(begin, GROUP)] * scales[b]).astype(BF16)
            next_ref[b, pl.ds(begin, GROUP)] = scaled
            parts.append(scaled.reshape(flat, columns))
        both = jnp.concatenate(parts, axis=1)
        term = jnp.dot(both, back_ref[0], preferred_element_type=F32)
        terms[step, pl.ds(begin, GROUP)] = term.reshape(GROUP, capacity, columns)

    @pl.when(step == kinds - 1)
    def _():
        for target, half in ((own_out, core), (other_out, 1 - core)):
            target[...] = jnp.zeros_like(target)

            @pl.loop(0, chips * share)
            def _(i):
                chip, channel = i // share, i % share
                at = (2 * chip + half) * share + channel
                loaded = [terms[j, at] for j in range(terms.shape[0])]
                merged = jnp.zeros((span, columns), F32)
                for k in range(2 * HALO):
                    tap_sum = taps_ref[0, k] * loaded[0]
                    for j in range(1, len(loaded)):
                        tap_sum += taps_ref[j, k] * loaded[j]
                    tail = jnp.zeros((span - capacity, columns), F32)
                    tall = jnp.concatenate([tap_sum, tail], 0)
                    merged += pltpu.roll(tall, k, 0) if k else tall
                target[chip, channel, pl.ds(base, span), :] = pltpu.roll(merged, shift, 0)


def prox(facts, taps, thresholds, own, other, ahead, back, dual):
    subbands, channels, capacity, columns = dual.shape
    kinds = subbands // 2
    smem = pl.BlockSpec(memory_space=pltpu.SMEM)
    vmem = pl.BlockSpec(memory_space=pltpu.VMEM)
    per_dict = pl.BlockSpec((1, 2 * columns, 2 * columns), lambda i: (i // 2, 0, 0))
    per_dict_back = pl.BlockSpec((1, 2 * columns, columns), lambda i: (i // 2, 0, 0))
    block = pl.BlockSpec((2, channels, capacity, columns), lambda i: (i, 0, 0, 0))
    return pl.pallas_call(
        prox_kernel,
        grid=(kinds,),
        out_shape=(
            jax.ShapeDtypeStruct(dual.shape, dual.dtype),
            jax.ShapeDtypeStruct(own.shape, F32),
            jax.ShapeDtypeStruct(own.shape, F32),
        ),
        in_specs=[smem, smem, smem, vmem, vmem, per_dict, per_dict_back, block],
        out_specs=(block, vmem, vmem),
        scratch_shapes=[
            pltpu.VMEM((channels, capacity + 8, columns), F32),
            pltpu.VMEM((kinds, channels, capacity, columns), F32),
            pltpu.VMEM((2, channels, capacity, columns), F32),
        ],
        compiler_params=pltpu.CompilerParams(vmem_limit_bytes=60 * 2**20),
    )(facts, taps, thresholds, own, other, ahead, back, dual)


def highpass(lowpass_row):
    tap_count = lowpass_row.shape[0]
    parity = jnp.where(jnp.arange(tap_count) % 2 == 0, 1.0, -1.0).astype(F32)
    return parity * lowpass_row[::-1]


def on_device(image_cube, dual, lowpass, thresholds, facet_rows):
    groups = lax.axis_size("fac")
    band_index = lax.axis_index("grp")
    facet_index = lax.axis_index("fac")
    _, band_rows, columns = image_cube.shape
    capacity = dual.shape[2]
    dicts, tap_count = lowpass.shape
    lows = lowpass.astype(F32)
    taps = jnp.stack([jnp.stack([lows[d], highpass(lows[d])]) for d in range(dicts)])
    place = jnp.arange(columns)
    offset = place[:, None] - place[None, :] + HALO
    matrix = jnp.zeros((dicts, 2, columns, columns), F32)
    for k in range(tap_count):
        matrix = matrix + jnp.where(offset == k, taps[:, :, k, None, None], 0.0)
    ahead = jnp.concatenate([matrix[:, 0], matrix[:, 1]], axis=2)
    ahead = jnp.concatenate([ahead, ahead], axis=1).astype(BF16)
    back = jnp.swapaxes(matrix, 2, 3).reshape(dicts, 2 * columns, columns).astype(BF16)
    row_taps = taps.reshape(2 * dicts, tap_count)

    lengths = lax.dynamic_index_in_dim(facet_rows, band_index, 0, keepdims=False)
    starts = jnp.cumsum(lengths) - lengths
    pairs = groups // 2
    pair_starts = starts[::2]
    core = facet_index % 2
    facet_offset = starts[facet_index] - starts[facet_index - core]
    facts = jnp.stack([core, facet_offset, lengths[facet_index]]).astype(jnp.int32)
    last_offset = band_rows - pair_starts[-1]

    above = shifted(image_cube[:, band_rows - HALO :], "grp", 1)
    below = shifted(image_cube[:, :HALO], "grp", -1)
    same_core = [list(range(c, groups, 2)) for c in range(2)]
    siblings = [(i, i ^ 1) for i in range(groups)]

    def run(cap):
        def body():
            sent = cut(pair_starts, image_cube, above, below, pairs, cap)
            own = lax.all_to_all(
                sent, "fac", split_axis=0, concat_axis=0, tiled=True, axis_index_groups=same_core
            )
            other = lax.ppermute(own, "fac", siblings)
            updated, own_out, other_out = prox(
                facts, row_taps, thresholds, own, other, ahead, back, dual
            )
            summed = own_out + lax.ppermute(other_out, "fac", siblings)
            windows = lax.all_to_all(
                summed, "fac", split_axis=0, concat_axis=0, tiled=True, axis_index_groups=same_core
            )
            spill_up = windows[0, :, :HALO]
            spill_down = lax.dynamic_slice_in_dim(windows[-1], HALO + last_offset, HALO, 1)
            from_next = shifted(spill_up, "grp", -1)
            from_previous = shifted(spill_down, "grp", 1)
            return updated, join(pair_starts, windows, from_previous, from_next, band_rows)

        return body

    most = jnp.max(facet_rows.reshape(-1, 2).sum(axis=1))
    mean = 2 * band_rows // groups
    steps = [mean, (mean + 2 * capacity) // 2, 2 * capacity]
    caps = [-(-(rows + 2 * HALO) // 8) * 8 for rows in steps]
    choice = (most > steps[0]).astype(jnp.int32) + (most > steps[1]).astype(jnp.int32)
    return lax.switch(choice, [run(cap) for cap in caps])


def solution(mesh):
    placed = (P("fac", "grp", None), P(None, None, ("grp", "fac"), None), P(), P(), P())
    return jax.shard_map(
        on_device,
        mesh=mesh,
        in_specs=placed,
        out_specs=(P(None, None, ("grp", "fac"), None), P("fac", "grp", None)),
        check_vma=False,
    )
```

time: 306 us -> 162 us (0.53)
  other arithmetic: 160 us -> 7.68 us
  blocking collectives: 0 us -> 43.9 us
  waiting for transfers between devices: 83 us -> 50.2 us
  Pallas kernels: 0 us -> 30.9 us
  local copies, waits for them, and re-layouts: 28.2 us -> 7.75 us
  starting transfers between devices: 28.1 us -> 15.7 us
    add x7 -> x2, other arithmetic: 85.7 us -> 3.37 us  [the longest x1 2.98 us: body(): summed = own_out + lax.ppermute(other_out, 'fac', siblings)]
    all_to_all x0 -> x1, blocking collectives: none -> 43.9 us  [body(): lax.all_to_all(sent, 'fac', split_axis=0, concat_axis=0, tiled=True, axis...]
    all_to_all x2 -> x1, waiting for transfers between devices: 81.2 us -> 38.4 us  [body(): lax.all_to_all(summed, 'fac', split_axis=0, concat_axis=0, tiled=True, ax...]
    reduce_sum x5 -> x1, other arithmetic: 37 us -> 0.12 us  [on_device(): most = jnp.max(facet_rows.reshape(-1, 2).sum(axis=1))]
    pallas_call x0 -> x3, Pallas kernels: none -> 30.9 us  [the longest x1 27 us: prox(): pl.pallas_call(prox_kernel, grid=(kinds,), out_shape=(jax.ShapeDtypeStruc...]
    gather x3 -> x0, local copies, waits for them, and re-layouts: 10.4 us -> none  [the longest x1 6.55 us: on_device(): picked = jnp.take(image_cube, jnp.clip(row_index, 0, band_rows - 1), axis=1)]
    unnamed x7 -> x0, other arithmetic: 10.3 us -> none
    ppermute x0 -> x2, waiting for transfers between devices: none -> 7.26 us  [the longest x1 3.67 us: body(): summed = own_out + lax.ppermute(other_out, 'fac', siblings)]
  transfers between devices with their start and end apart: 6 -> 7, of which waited for: 3 -> 4; matrix products, arithmetic and copies ran while one was open for 9% -> 6% of each run, Pallas kernels for 0% -> 0%
where the time goes in v1:
time: 162 us; the launch traced here: 161 us
  waiting for transfers between devices  50.2 us (31%)
  blocking collectives  43.9 us (27%)
  Pallas kernels  30.9 us (19%)
  starting transfers between devices  15.7 us (10%)
  local copies, waits for them, and re-layouts  7.75 us (5%)
  other arithmetic  7.68 us (5%)
  between operations  3.44 us (2%)
    all_to_all x1, blocking collectives, body(): lax.all_to_all(sent, 'fac', split_axis=0, concat_axis=0, tiled=True, axis...  43.9 us
    all_to_all x1, waiting for transfers between devices, body(): lax.all_to_all(summed, 'fac', split_axis=0, concat_axis=0, tiled=True, ax...  38.4 us
    pallas_call x1, Pallas kernels, prox(): pl.pallas_call(prox_kernel, grid=(kinds,), out_shape=(jax.ShapeDtypeStruc...  27 us
    ppermute x4, starting transfers between devices, shifted(): return lax.ppermute(x, axis, pairs)  12 us
    ppermute x4, waiting for transfers between devices, shifted(): return lax.ppermute(x, axis, pairs)  4.51 us
    ppermute x1, waiting for transfers between devices, body(): summed = own_out + lax.ppermute(other_out, 'fac', siblings)  3.67 us
    ppermute x1, waiting for transfers between devices, body(): other = lax.ppermute(own, 'fac', siblings)  3.59 us
    all_to_all x1, starting transfers between devices, body(): lax.all_to_all(summed, 'fac', split_axis=0, concat_axis=0, tiled=True, ax...  3.57 us
  transfers between devices with their start and end apart: 7, of which 4 were waited for; matrix products, arithmetic and copies ran while one was open for 6% of the time, Pallas kernels for 0%

profile of v1, /device:TPU:4, one launch (start us, length us, event | category | flops | bytes accessed | tf_op | source)
XLA Modules:
  0.0 161.0 jit_solution(11311146656010045840)
XLA Ops:
  0.6 0.8 fusion.17
  1.4 3.3 %collective-permute-start.13 = (f32[4,2,256]{2,1,0:T(2,128)S(1)}, f32[4,2,256]{2,1,0:T(2,128)S(1)}, u32[]{:S(2)}, u32[]{:S(2)}) collective-permute-start(f32[4,2,256]{2,1,0:T(2,128)S(1)} %get-tuple-element.145), channel_id=1, source_target_pairs={{8,0},{16,8},{24,16},{9,1},{17,9},{25,17},{10,2},{18,10},{26,18},{... | collective-permute-start | bytes 24584 | tf_op jit(solution)/shard_map/ppermute | solution.py:19
  4.8 2.5 %collective-permute-start.12 = (f32[4,2,256]{2,1,0:T(2,128)S(1)}, f32[4,2,256]{2,1,0:T(2,128)S(1)}, u32[]{:S(2)}, u32[]{:S(2)}) collective-permute-start(f32[4,2,256]{2,1,0:T(2,128)S(1)} %get-tuple-element.146), channel_id=1, source_target_pairs={{0,8},{8,16},{16,24},{1,9},{9,17},{17,25},{2,10},{10,18},{18,26},{... | collective-permute-start | bytes 24584 | tf_op jit(solution)/shard_map/ppermute | solution.py:19
  7.3 0.7 convert_element_type.15
  7.9 0.7 fusion.18
  10.1 0.7 fusion.16
  10.9 0.7 bitcast_subtract_fusion
  15.0 0.7 add_convert_fusion
  15.7 0.7 pad_add_fusion
  18.6 142.3 %conditional.1 = (bf16[8,32,72,256]{3,2,1,0:T(8,128)(2,1)}, f32[4,384,256]{2,1,0:T(8,128)}) conditional(s32[]{:T(128)} %clamp.7, (s32[8]{0:T(128)S(1)}, f32[4,384,256]{2,1,0:T(8,128)S(1)}, f32[4,2,256]{2,1,0:T(2,128)S(1)}, f32[4,2,256]{2,1,0:T(2,128)S(1)}, s32[3]{0:T(128)S(1)}, /*index=5*/f32[2,2,4]{2,1,0:T(2,128)S(1)}, ...), branch_computations={%region_3.4_spmd, %region_4.5_spmd, %region_5.6_spmd} | conditional | flops 622596 | bytes 61112672 | solution.py:272
  18.7 1.3 branch_0_fun.3
  20.0 43.9 %all_to_all.24.own_ref = f32[4,4,104,256]{3,2,1,0:T(8,128)S(1)} all-to-all(f32[4,4,104,256]{3,2,1,0:T(8,128)S(1)} %branch_0_fun.3), channel_id=1, replica_groups={{0,2,4,6},{1,3,5,7},{8,10,12,14},{9,11,13,15},{16,18,20,22},{17,19,21,2..., dimensions={0} | all-to-all | bytes 3407872 | tf_op jit(solution)/shard_map/cond/branch_0_fun/all_to_all | solution.py:248
  63.9 1.2 copy-done.3
  65.1 3.6 %collective-permute-done.other_ref = f32[4,4,104,256]{3,2,1,0:T(8,128)S(1)} collective-permute-done((f32[4,4,104,256]{3,2,1,0:T(8,128)S(1)}, f32[4,4,104,256]{3,2,1,0:T(8,128)S(1)}, u32[]{:S(2)}, u32[]{:S(2)}) %collective-permute-start) | collective-permute-done | bytes 1703968 | tf_op jit(solution)/shard_map/cond/branch_0_fun/ppermute | solution.py:251
  68.7 1.2 copy-done.6
  69.9 27.0 %branch_0_fun.4 = (bf16[8,32,72,256]{3,2,1,0:T(8,128)(2,1)}, f32[4,4,104,256]{3,2,1,0:T(8,128)}, f32[4,4,104,256]{3,2,1,0:T(8,128)}) custom-call(s32[3]{0:T(128)S(1)} %get-tuple-element.66.facts_ref, f32[4,4]{1,0:T(4,128)S(1)} %bitcast.65, f32[8]{0:T(128)S(1)} %get-tuple-element.123.thresholds_ref, f32[4,4,104,256]{3,2,1,0:T(8,128)} %copy-done.3, ...), custom_call_target="tpu_custom_call" | custom-call | tf_op jit(solution)/shard_map/cond/branch_0_fun/pallas_call | solution.py:187
  97.1 3.7 %collective-permute-done.1 = f32[4,4,104,256]{3,2,1,0:T(8,128)S(1)} collective-permute-done((f32[4,4,104,256]{3,2,1,0:T(8,128)}, f32[4,4,104,256]{3,2,1,0:T(8,128)S(1)}, u32[]{:S(2)}, u32[]{:S(2)}) %collective-permute-start.1) | collective-permute-done | bytes 1703968 | tf_op jit(solution)/shard_map/cond/branch_0_fun/ppermute | solution.py:255
  100.8 3.0 %add.75 = f32[4,4,104,256]{3,2,1,0:T(8,128)} add(f32[4,4,104,256]{3,2,1,0:T(8,128)} %get-tuple-element.77, f32[4,4,104,256]{3,2,1,0:T(8,128)S(1)} %collective-permute-done.1) | non-fusion elementwise | flops 425984 | bytes 5111808 | tf_op jit(solution)/shard_map/cond/branch_0_fun/add | solution.py:255
  103.7 3.6 %all-to-all-start.1 = ((f32[4,4,104,256]{3,2,1,0:T(8,128)}), f32[4,4,104,256]{3,2,1,0:T(8,128)S(1)}, u32[]{:S(2)}, u32[]{:S(2)}) async-start(f32[4,4,104,256]{3,2,1,0:T(8,128)} %add.75), calls=%async_computation.1 | async-start | bytes 3407872 | tf_op jit(solution)/shard_map/cond/branch_0_fun/all_to_all | solution.py:256
  109.2 38.4 %all-to-all-done.1.windows_ref = f32[4,4,104,256]{3,2,1,0:T(8,128)S(1)} async-done(((f32[4,4,104,256]{3,2,1,0:T(8,128)}), f32[4,4,104,256]{3,2,1,0:T(8,128)S(1)}, u32[]{:S(2)}, u32[]{:S(2)}) %all-to-all-start.1) | async-done | bytes 1703968 | tf_op jit(solution)/shard_map/cond/branch_0_fun/all_to_all | solution.py:256
  147.6 4.2 %collective-permute-start.3 = (f32[4,2,256]{2,1,0:T(2,128)S(1)}, f32[4,2,256]{2,1,0:T(2,128)S(1)}, u32[]{:S(2)}, u32[]{:S(2)}) collective-permute-start(f32[4,2,256]{2,1,0:T(2,128)S(1)} %slice_bitcast_fusion), channel_id=1, source_target_pairs={{8,0},{16,8},{24,16},{9,1},{17,9},{25,17},{10,2},{18,10},{26,18},{... | collective-permute-start | bytes 24584 | tf_op jit(solution)/shard_map/cond/branch_0_fun/ppermute | solution.py:19
  151.9 1.9 %collective-permute-start.2 = (f32[4,2,256]{2,1,0:T(2,128)S(1)}, f32[4,2,256]{2,1,0:T(2,128)S(1)}, u32[]{:S(2)}, u32[]{:S(2)}) collective-permute-start(f32[4,2,256]{2,1,0:T(2,128)S(1)} %dynamic-slice_bitcast_fusion), channel_id=1, source_target_pairs={{0,8},{8,16},{16,24},{1,9},{9,17},{17,25},{2,10},{10,18},{18,26},{... | collective-permute-start | bytes 24584 | tf_op jit(solution)/shard_map/cond/branch_0_fun/ppermute | solution.py:19
  153.9 4.5 %collective-permute-done.2.above_ref = f32[4,2,256]{2,1,0:T(2,128)S(1)} collective-permute-done((f32[4,2,256]{2,1,0:T(2,128)S(1)}, f32[4,2,256]{2,1,0:T(2,128)S(1)}, u32[]{:S(2)}, u32[]{:S(2)}) %collective-permute-start.2) | collective-permute-done | bytes 8224 | tf_op jit(solution)/shard_map/cond/branch_0_fun/ppermute | solution.py:19
  158.4 2.6 %branch_0_fun.5 = f32[4,384,256]{2,1,0:T(8,128)} custom-call(s32[4]{0:T(128)S(1)} %slice.71.starts_ref, f32[4,4,104,256]{3,2,1,0:T(8,128)S(1)} %all-to-all-done.1.windows_ref, f32[4,2,256]{2,1,0:T(2,128)S(1)} %collective-permute-done.2.above_ref, f32[4,2,256]{2,1,0:T(2,128)S(1)} %collective-permute-done.3.below_ref), custom_call_target="tpu_custom_call" | custom-call | tf_op jit(solution)/shard_map/cond/branch_0_fun/pallas_call | solution.py:80
  (58 shorter events, 5.2 us)
Async XLA Ops:
  1.4 17.2 %collective-permute-start.13 = (f32[4,2,256]{2,1,0:T(2,128)S(1)}, f32[4,2,256]{2,1,0:T(2,128)S(1)}, u32[]{:S(2)}, u32[]{:S(2)}) collective-permute-start(f32[4,2,256]{2,1,0:T(2,128)S(1)} %get-tuple-element.145), channel_id=1, source_target_pairs={{8,0},{16,8},{24,16},{9,1},{17,9},{25,17},{10,2},{18,10},{26,18},{... | collective-permute-start | bytes 24584 | tf_op jit(solution)/shard_map/ppermute | solution.py:19
  4.8 13.8 %collective-permute-start.12 = (f32[4,2,256]{2,1,0:T(2,128)S(1)}, f32[4,2,256]{2,1,0:T(2,128)S(1)}, u32[]{:S(2)}, u32[]{:S(2)}) collective-permute-start(f32[4,2,256]{2,1,0:T(2,128)S(1)} %get-tuple-element.146), channel_id=1, source_target_pairs={{0,8},{8,16},{16,24},{1,9},{9,17},{17,25},{2,10},{10,18},{18,26},{... | collective-permute-start | bytes 24584 | tf_op jit(solution)/shard_map/ppermute | solution.py:19
  11.6 0.7 copy-start.8
  12.1 6.5 %copy-start = (f32[4,384,256]{2,1,0:T(8,128)S(1)}, f32[4,384,256]{2,1,0:T(8,128)}, u32[]{:S(2)}) copy-start(f32[4,384,256]{2,1,0:T(8,128)} %param.8) | copy-start | bytes 4718596
  12.1 6.5 %copy-start.7 = (f32[8]{0:T(128)S(1)}, f32[8]{0:T(128)}, u32[]{:S(2)}) copy-start(f32[8]{0:T(128)} %param.11) | copy-start | bytes 100
  63.9 1.2 copy-start.3
  65.1 3.6 %collective-permute-start = (f32[4,4,104,256]{3,2,1,0:T(8,128)S(1)}, f32[4,4,104,256]{3,2,1,0:T(8,128)S(1)}, u32[]{:S(2)}, u32[]{:S(2)}) collective-permute-start(f32[4,4,104,256]{3,2,1,0:T(8,128)S(1)} %all_to_all.24.own_ref), channel_id=1, source_target_pairs={{0,1},{1,0},{2,3},{3,2},{4,5},{5,4},{6,7},{7,6},{8,9},{9,8},{10,11... | collective-permute-start | bytes 5111816 | tf_op jit(solution)/shard_map/cond/branch_0_fun/ppermute | solution.py:251
  68.7 1.2 copy-start.6
  96.9 3.8 %collective-permute-start.1 = (f32[4,4,104,256]{3,2,1,0:T(8,128)}, f32[4,4,104,256]{3,2,1,0:T(8,128)S(1)}, u32[]{:S(2)}, u32[]{:S(2)}) collective-permute-start(f32[4,4,104,256]{3,2,1,0:T(8,128)} %get-tuple-element.78), channel_id=1, source_target_pairs={{0,1},{1,0},{2,3},{3,2},{4,5},{5,4},{6,7},{7,6},{8,9},{9,8},{10,11... | collective-permute-start | bytes 5111816 | tf_op jit(solution)/shard_map/cond/branch_0_fun/ppermute | solution.py:255
  103.7 43.9 %all-to-all-start.1 = ((f32[4,4,104,256]{3,2,1,0:T(8,128)}), f32[4,4,104,256]{3,2,1,0:T(8,128)S(1)}, u32[]{:S(2)}, u32[]{:S(2)}) async-start(f32[4,4,104,256]{3,2,1,0:T(8,128)} %add.75), calls=%async_computation.1 | async-start | bytes 3407872 | tf_op jit(solution)/shard_map/cond/branch_0_fun/all_to_all | solution.py:256
  147.6 6.2 %collective-permute-start.3 = (f32[4,2,256]{2,1,0:T(2,128)S(1)}, f32[4,2,256]{2,1,0:T(2,128)S(1)}, u32[]{:S(2)}, u32[]{:S(2)}) collective-permute-start(f32[4,2,256]{2,1,0:T(2,128)S(1)} %slice_bitcast_fusion), channel_id=1, source_target_pairs={{8,0},{16,8},{24,16},{9,1},{17,9},{25,17},{10,2},{18,10},{26,18},{... | collective-permute-start | bytes 24584 | tf_op jit(solution)/shard_map/cond/branch_0_fun/ppermute | solution.py:19
  151.9 6.4 %collective-permute-start.2 = (f32[4,2,256]{2,1,0:T(2,128)S(1)}, f32[4,2,256]{2,1,0:T(2,128)S(1)}, u32[]{:S(2)}, u32[]{:S(2)}) collective-permute-start(f32[4,2,256]{2,1,0:T(2,128)S(1)} %dynamic-slice_bitcast_fusion), channel_id=1, source_target_pairs={{0,8},{8,16},{16,24},{1,9},{9,17},{17,25},{2,10},{10,18},{18,26},{... | collective-permute-start | bytes 24584 | tf_op jit(solution)/shard_map/cond/branch_0_fun/ppermute | solution.py:19

commit v2 on v1

v2 whole, which is shorter than its diff:
```python
import functools

import jax
import jax.numpy as jnp
from jax import lax
from jax.experimental import pallas as pl
from jax.experimental.pallas import tpu as pltpu
from jax.sharding import PartitionSpec as P

HALO = 2
LEAD = 8
F32 = jnp.float32
BF16 = jnp.bfloat16
MESH = pl.DeviceIdType.MESH


def shifted(x, axis, by):
    devices = lax.axis_size(axis)
    pairs = [(i, i + by) for i in range(devices) if 0 <= i + by < devices]
    return lax.ppermute(x, axis, pairs)


def facet_starts(rows_ref):
    band = lax.axis_index("grp")
    starts = [jnp.int32(0)]
    for facet in range(rows_ref.shape[1]):
        starts.append(starts[-1] + rows_ref[band, facet])
    return starts


def cut_kernel(cap, rows_ref, image_ref, above_ref, below_ref, out_ref, padded):
    rows = image_ref.shape[1]
    padded[:, 0:LEAD, :] = jnp.zeros_like(padded[:, 0:LEAD, :])
    tail = padded.shape[1] - LEAD - rows
    padded[:, LEAD + rows :, :] = jnp.zeros((padded.shape[0], tail, padded.shape[2]), F32)
    padded[:, LEAD : LEAD + rows, :] = image_ref[...]
    padded[:, LEAD - HALO : LEAD, :] = above_ref[...]
    padded[:, LEAD + rows : LEAD + rows + HALO, :] = below_ref[...]
    starts = facet_starts(rows_ref)

    for pair in range(out_ref.shape[0]):
        begin = starts[2 * pair] + (LEAD - HALO)
        base = pl.multiple_of((begin // 8) * 8, 8)
        turn = cap + 8 - (begin - base)

        @pl.loop(0, out_ref.shape[1])
        def _(channel):
            window = padded[channel, pl.ds(base, cap + 8), :]
            out_ref[pair, channel] = pltpu.roll(window, turn, 0)[:cap]


def cut(facet_rows, image, above, below, pairs, cap):
    channels, rows, columns = image.shape
    vmem = pl.BlockSpec(memory_space=pltpu.VMEM)
    return pl.pallas_call(
        functools.partial(cut_kernel, cap),
        out_shape=jax.ShapeDtypeStruct((pairs, channels, cap, columns), F32),
        in_specs=[pl.BlockSpec(memory_space=pltpu.SMEM), vmem, vmem, vmem],
        out_specs=vmem,
        scratch_shapes=[pltpu.VMEM((channels, LEAD + rows + cap + 16, columns), F32)],
        compiler_params=pltpu.CompilerParams(vmem_limit_bytes=48 * 2**20),
    )(facet_rows, image, above, below)


def join_kernel(cap, rows_ref, windows_ref, above_ref, below_ref, out_ref, padded):
    rows = out_ref.shape[1]
    padded[...] = jnp.zeros_like(padded)
    starts = facet_starts(rows_ref)

    for pair in range(windows_ref.shape[0]):
        begin = starts[2 * pair] + (LEAD - HALO)
        base = pl.multiple_of((begin // 8) * 8, 8)

        @pl.loop(0, windows_ref.shape[1])
        def _(channel):
            window = windows_ref[pair, channel]
            window = jnp.concatenate([window, jnp.zeros((8, window.shape[1]), F32)], 0)
            here = (channel, pl.ds(base, cap + 8), slice(None))
            padded[here] = padded[here] + pltpu.roll(window, begin - base, 0)

    out_ref[...] = padded[:, LEAD : LEAD + rows, :]
    out_ref[:, 0:HALO, :] = out_ref[:, 0:HALO, :] + above_ref[...]
    out_ref[:, rows - HALO : rows, :] = out_ref[:, rows - HALO : rows, :] + below_ref[...]


def join(facet_rows, windows, above, below, rows):
    pairs, channels, cap, columns = windows.shape
    vmem = pl.BlockSpec(memory_space=pltpu.VMEM)
    return pl.pallas_call(
        functools.partial(join_kernel, cap),
        out_shape=jax.ShapeDtypeStruct((channels, rows, columns), F32),
        in_specs=[pl.BlockSpec(memory_space=pltpu.SMEM), vmem, vmem, vmem],
        out_specs=vmem,
        scratch_shapes=[pltpu.VMEM((channels, LEAD + rows + cap + 16, columns), F32)],
        compiler_params=pltpu.CompilerParams(vmem_limit_bytes=48 * 2**20),
    )(facet_rows, windows, above, below)


def position(chips):
    facet = lax.axis_index("fac")
    core = lax.rem(facet, 2)
    chip = lax.div(facet, 2)
    sibling = facet + 1 - 2 * core

    def at(r):
        return lax.rem(chip + r, chips)

    return core, chip, sibling, at


def greet(core, sibling, at, chips):
    barrier = pltpu.get_barrier_semaphore()
    for device in [2 * at(r) + core for r in range(1, chips)] + [sibling]:
        pl.semaphore_signal(barrier, inc=1, device_id={"fac": device}, device_id_type=MESH)
    pl.semaphore_wait(barrier, chips)


def remote(source, target, send, recv, device):
    return pltpu.make_async_remote_copy(
        src_ref=source, dst_ref=target, send_sem=send, recv_sem=recv,
        device_id={"fac": device}, device_id_type=MESH,
    )


def spread_kernel(sent, own, other, send, recv, pass_send, pass_recv, kept):
    chips, share = sent.shape[:2]
    core, chip, sibling, at = position(chips)
    greet(core, sibling, at, chips)
    home = pltpu.make_async_copy(sent.at[chip], own.at[chip], kept)
    home.start()
    outgoing, passed = [], []
    for c in range(share):
        for r in range(1, chips):
            outgoing.append(remote(
                sent.at[at(r), c], own.at[chip, c], send.at[r, c], recv.at[r, c],
                2 * at(r) + core,
            ))
            outgoing[-1].start()
        passed.append(remote(
            sent.at[chip, c], other.at[chip, c], pass_send.at[0, c], pass_recv.at[0, c], sibling
        ))
        passed[-1].start()
    for c in range(share):
        for r in range(1, chips):
            outgoing[c * (chips - 1) + r - 1].wait_recv()
            source = at(chips - r)
            passed.append(remote(
                own.at[source, c], other.at[source, c], pass_send.at[r, c], pass_recv.at[r, c],
                sibling,
            ))
            passed[-1].start()
    for copy in outgoing:
        copy.wait_send()
    for copy in passed:
        copy.wait()
    home.wait()


def spread(sent, collective_id):
    chips, share = sent.shape[:2]
    vmem = pl.BlockSpec(memory_space=pltpu.VMEM)
    shape = jax.ShapeDtypeStruct(sent.shape, F32)
    return pl.pallas_call(
        spread_kernel,
        out_shape=(shape, shape),
        in_specs=[vmem],
        out_specs=(vmem, vmem),
        scratch_shapes=[pltpu.SemaphoreType.DMA((chips, share))] * 4 + [pltpu.SemaphoreType.DMA],
        compiler_params=pltpu.CompilerParams(
            collective_id=collective_id, has_side_effects=True, vmem_limit_bytes=48 * 2**20
        ),
    )(sent)


def collect_kernel(own, other, out, arrived, total, send, recv, pass_send, pass_recv):
    chips, share = own.shape[:2]
    core, chip, sibling, at = position(chips)
    greet(core, sibling, at, chips)
    passed, outgoing = [], []
    order = [(c, r) for c in range(share) for r in list(range(1, chips)) + [0]]
    for c, r in order:
        passed.append(remote(
            other.at[at(r), c], arrived.at[at(r), c], pass_send.at[r, c], pass_recv.at[r, c],
            sibling,
        ))
        passed[-1].start()
    for copy, (c, r) in zip(passed, order):
        copy.wait_recv()
        summed = own[at(r), c] + arrived[at(r), c]
        if r == 0:
            out[chip, c] = summed
        else:
            total[at(r), c] = summed
            outgoing.append(remote(
                total.at[at(r), c], out.at[chip, c], send.at[r, c], recv.at[r, c],
                2 * at(r) + core,
            ))
            outgoing[-1].start()
    for copy in passed:
        copy.wait_send()
    for copy in outgoing:
        copy.wait()


def collect(own, other, collective_id):
    chips, share = own.shape[:2]
    vmem = pl.BlockSpec(memory_space=pltpu.VMEM)
    return pl.pallas_call(
        collect_kernel,
        out_shape=jax.ShapeDtypeStruct(own.shape, F32),
        in_specs=[vmem, vmem],
        out_specs=vmem,
        scratch_shapes=[pltpu.VMEM(own.shape, F32)] * 2
        + [pltpu.SemaphoreType.DMA((chips, share))] * 4,
        compiler_params=pltpu.CompilerParams(
            collective_id=collective_id, has_side_effects=True, vmem_limit_bytes=48 * 2**20
        ),
    )(own, other)


GROUP = 8


def tap(low_ref, d, a, k):
    count = low_ref.shape[1]
    high = low_ref[d, count - 1 - k] * (1.0 if k % 2 == 0 else -1.0)
    return jnp.where(a == 0, low_ref[d, k], high)


def prox_kernel(
    rows_ref, low_ref, thresholds_ref, own_ref, other_ref, dual_ref,
    next_ref, own_out, other_out, image, terms, wide, ahead, back,
):
    step = pl.program_id(0)
    kinds = pl.num_programs(0)
    d, a = step // 2, step % 2
    facet, band = lax.axis_index("fac"), lax.axis_index("grp")
    core = facet % 2
    offset = jnp.where(core == 0, 0, rows_ref[band, facet - core])
    length = rows_ref[band, facet]
    channels, capacity, columns = dual_ref.shape[1:]
    chips, share, cap, _ = own_ref.shape
    span = capacity + 16
    base = pl.multiple_of(jnp.minimum((offset // 8) * 8, cap - span), 8)
    shift = offset - base
    flat = GROUP * capacity

    @pl.when(a == 0)
    def _():
        into = lax.broadcasted_iota(jnp.int32, (columns, columns), 0)
        of = lax.broadcasted_iota(jnp.int32, (columns, columns), 1)
        for b in range(2):
            forward = jnp.zeros((columns, columns), F32)
            adjoint = jnp.zeros((columns, columns), F32)
            for k in range(2 * HALO):
                value = tap(low_ref, d, b, k)
                forward = jnp.where(into - of + HALO == k, value, forward)
                adjoint = jnp.where(of - into + HALO == k, value, adjoint)
            forward = forward.astype(BF16)
            ahead[0:columns, b * columns : (b + 1) * columns] = forward
            ahead[columns:, b * columns : (b + 1) * columns] = forward
            back[b * columns : (b + 1) * columns, :] = adjoint.astype(BF16)

    @pl.when(step == 0)
    def _():
        for source, half in ((own_ref, core), (other_ref, 1 - core)):
            @pl.loop(0, chips * share)
            def _(i):
                chip, channel = i // share, i % share
                window = source[chip, channel, pl.ds(base, span), :]
                turned = pltpu.roll(window, span - shift, 0)
                image[(2 * chip + half) * share + channel] = turned[: capacity + 8]

    keep = lax.broadcasted_iota(jnp.int32, (capacity, columns), 0) < length

    def analysis(group, sums):
        begin = pl.multiple_of(group * GROUP, GROUP)
        rows = tap(low_ref, d, a, 0) * image[pl.ds(begin, GROUP), 0:capacity, :]
        for k in range(1, 2 * HALO):
            rows += tap(low_ref, d, a, k) * image[pl.ds(begin, GROUP), k : k + capacity, :]
        rows = rows.reshape(flat, columns)
        high = rows.astype(BF16)
        low = (rows - high.astype(F32)).astype(BF16)
        both = jnp.concatenate([high, low], axis=1)
        coefficient = jnp.dot(both, ahead[...], preferred_element_type=F32)
        out = []
        for b in range(2):
            part = coefficient[:, b * columns : (b + 1) * columns]
            part = part.reshape(GROUP, capacity, columns)
            u = dual_ref[b, pl.ds(begin, GROUP)].astype(F32) + part
            u = jnp.where(keep, u, 0.0)
            wide[b, pl.ds(begin, GROUP)] = u
            out.append(sums[b] + jnp.sum(u * u, axis=0))
        return tuple(out)

    zero = jnp.zeros((capacity, columns), F32)
    sums = lax.fori_loop(0, channels // GROUP, analysis, (zero, zero))
    scales = []
    for b in range(2):
        radius = thresholds_ref[2 * step + b]
        scales.append(radius / jnp.maximum(jnp.sqrt(sums[b]), radius))

    @pl.loop(0, channels // GROUP)
    def _(group):
        begin = pl.multiple_of(group * GROUP, GROUP)
        parts = []
        for b in range(2):
            scaled = (wide[b, pl.ds(begin, GROUP)] * scales[b]).astype(BF16)
            next_ref[b, pl.ds(begin, GROUP)] = scaled
            parts.append(scaled.reshape(flat, columns))
        both = jnp.concatenate(parts, axis=1)
        term = jnp.dot(both, back[...], preferred_element_type=F32)
        terms[step, pl.ds(begin, GROUP)] = term.reshape(GROUP, capacity, columns)

    @pl.when(step == kinds - 1)
    def _():
        for target, half in ((own_out, core), (other_out, 1 - core)):
            target[...] = jnp.zeros_like(target)

            @pl.loop(0, chips * share)
            def _(i):
                chip, channel = i // share, i % share
                at = (2 * chip + half) * share + channel
                loaded = [terms[j, at] for j in range(terms.shape[0])]
                merged = jnp.zeros((span, columns), F32)
                for k in range(2 * HALO):
                    tap_sum = tap(low_ref, 0, 0, k) * loaded[0]
                    for j in range(1, len(loaded)):
                        tap_sum += tap(low_ref, j // 2, j % 2, k) * loaded[j]
                    tail = jnp.zeros((span - capacity, columns), F32)
                    tall = jnp.concatenate([tap_sum, tail], 0)
                    merged += pltpu.roll(tall, k, 0) if k else tall
                target[chip, channel, pl.ds(base, span), :] = pltpu.roll(merged, shift, 0)


def prox(facet_rows, lows, thresholds, own, other, dual):
    subbands, channels, capacity, columns = dual.shape
    kinds = subbands // 2
    smem = pl.BlockSpec(memory_space=pltpu.SMEM)
    vmem = pl.BlockSpec(memory_space=pltpu.VMEM)
    block = pl.BlockSpec((2, channels, capacity, columns), lambda i: (i, 0, 0, 0))
    return pl.pallas_call(
        prox_kernel,
        grid=(kinds,),
        out_shape=(
            jax.ShapeDtypeStruct(dual.shape, dual.dtype),
            jax.ShapeDtypeStruct(own.shape, F32),
            jax.ShapeDtypeStruct(own.shape, F32),
        ),
        in_specs=[smem, smem, smem, vmem, vmem, block],
        out_specs=(block, vmem, vmem),
        scratch_shapes=[
            pltpu.VMEM((channels, capacity + 8, columns), F32),
            pltpu.VMEM((kinds, channels, capacity, columns), F32),
            pltpu.VMEM((2, channels, capacity, columns), F32),
            pltpu.VMEM((2 * columns, 2 * columns), BF16),
            pltpu.VMEM((2 * columns, columns), BF16),
        ],
        compiler_params=pltpu.CompilerParams(vmem_limit_bytes=60 * 2**20),
    )(facet_rows, lows, thresholds, own, other, dual)


def on_device(image_cube, dual, lowpass, thresholds, facet_rows):
    groups = lax.axis_size("fac")
    band_index = lax.axis_index("grp")
    _, band_rows, columns = image_cube.shape
    capacity = dual.shape[2]
    pairs = groups // 2
    lows = lowpass.astype(F32)
    above = shifted(image_cube[:, band_rows - HALO :], "grp", 1)
    below = shifted(image_cube[:, :HALO], "grp", -1)

    def run(choice, cap):
        def body():
            sent = cut(facet_rows, image_cube, above, below, pairs, cap)
            own, other = spread(sent, 2 * choice)
            updated, own_out, other_out = prox(facet_rows, lows, thresholds, own, other, dual)
            windows = collect(own_out, other_out, 2 * choice + 1)
            spill_up = windows[0, :, :HALO]
            last_rows = facet_rows[band_index, -2] + facet_rows[band_index, -1]
            spill_down = lax.dynamic_slice_in_dim(windows[-1], HALO + last_rows, HALO, 1)
            from_next = shifted(spill_up, "grp", -1)
            from_previous = shifted(spill_down, "grp", 1)
            return updated, join(facet_rows, windows, from_previous, from_next, band_rows)

        return body

    most = jnp.max(facet_rows[:, ::2] + facet_rows[:, 1::2]) + 2 * HALO
    mean = 2 * band_rows // groups
    steps = [mean, (mean + 2 * capacity) // 2, 2 * capacity]
    caps = [-(-(rows + 2 * HALO) // 8) * 8 for rows in steps]
    choice = (most > caps[0]).astype(jnp.int32) + (most > caps[1]).astype(jnp.int32)
    return lax.switch(choice, [run(i, cap) for i, cap in enumerate(caps)])


def solution(mesh):
    placed = (P("fac", "grp", None), P(None, None, ("grp", "fac"), None), P(), P(), P())
    return jax.shard_map(
        on_device,
        mesh=mesh,
        in_specs=placed,
        out_specs=(P(None, None, ("grp", "fac"), None), P("fac", "grp", None)),
        check_vma=False,
    )
```

time: 162 us -> 145 us (0.90)
  Pallas kernels: 30.9 us -> 115 us
  waiting for transfers between devices: 50.2 us -> 4.84 us
  blocking collectives: 43.9 us -> 0 us
  other arithmetic: 7.68 us -> 1.29 us
  starting transfers between devices: 15.7 us -> 11.7 us
  between operations: 3.44 us -> 1.32 us
    pallas_call x0 -> x2, Pallas kernels: none -> 82.4 us  [the longest x1 41.3 us: spread(): pl.pallas_call(spread_kernel, out_shape=(shape, shape), in_specs=[vmem],...]
    all_to_all x1 -> x0, blocking collectives: 43.9 us -> none  [body(): lax.all_to_all(sent, 'fac', split_axis=0, concat_axis=0, tiled=True, axis...]
    all_to_all x1 -> x0, waiting for transfers between devices: 38.4 us -> none  [body(): lax.all_to_all(summed, 'fac', split_axis=0, concat_axis=0, tiled=True, ax...]
    ppermute x2 -> x0, waiting for transfers between devices: 7.26 us -> none  [the longest x1 3.67 us: body(): summed = own_out + lax.ppermute(other_out, 'fac', siblings)]
    all_to_all x1 -> x0, starting transfers between devices: 3.57 us -> none  [body(): lax.all_to_all(summed, 'fac', split_axis=0, concat_axis=0, tiled=True, ax...]
    add x2 -> x0, other arithmetic: 3.37 us -> none  [the longest x1 2.98 us: body(): summed = own_out + lax.ppermute(other_out, 'fac', siblings)]
    cond x4 -> x12, local copies, waits for them, and re-layouts: 2.38 us -> 5.31 us
  transfers between devices with their start and end apart: 7 -> 4, of which waited for: 4 -> 2; matrix products, arithmetic and copies ran while one was open for 6% -> 2% of each run, Pallas kernels for 0% -> 0%
where the time goes in v2:
time: 145 us; the launch traced here: 143 us
  Pallas kernels  115 us (79%)
  starting transfers between devices  11.7 us (8%)
  local copies, waits for them, and re-layouts  8.31 us (6%)
  waiting for transfers between devices  4.84 us (3%)
    pallas_call x1, Pallas kernels, spread(): pl.pallas_call(spread_kernel, out_shape=(shape, shape), in_specs=[vmem],...  41.3 us
    pallas_call x1, Pallas kernels, collect(): pl.pallas_call(collect_kernel, out_shape=jax.ShapeDtypeStruct(own.shape,...  41.1 us
    pallas_call x1, Pallas kernels, prox(): pl.pallas_call(prox_kernel, grid=(kinds,), out_shape=(jax.ShapeDtypeStruc...  27.6 us
    ppermute x4, starting transfers between devices, shifted(): return lax.ppermute(x, axis, pairs)  11.7 us
    cond x12, local copies, waits for them, and re-layouts  5.31 us
    ppermute x4, waiting for transfers between devices, shifted(): return lax.ppermute(x, axis, pairs)  4.84 us
  transfers between devices with their start and end apart: 4, of which 2 were waited for; matrix products, arithmetic and copies ran while one was open for 2% of the time, Pallas kernels for 0%

profile of v2, /device:TPU:4, one launch (start us, length us, event | category | flops | bytes accessed | tf_op | source)
XLA Modules:
  0.0 143.4 jit_solution(15478073556134857982)
XLA Ops:
  0.6 0.8 fusion
  1.4 3.3 %collective-permute-start.7 = (f32[4,2,256]{2,1,0:T(2,128)S(1)}, f32[4,2,256]{2,1,0:T(2,128)S(1)}, u32[]{:S(2)}, u32[]{:S(2)}) collective-permute-start(f32[4,2,256]{2,1,0:T(2,128)S(1)} %get-tuple-element.108), channel_id=1, source_target_pairs={{8,0},{16,8},{24,16},{9,1},{17,9},{25,17},{10,2},{18,10},{26,18},{... | collective-permute-start | bytes 24584 | tf_op jit(solution)/shard_map/ppermute | solution.py:20
  4.8 2.5 %collective-permute-start.6 = (f32[4,2,256]{2,1,0:T(2,128)S(1)}, f32[4,2,256]{2,1,0:T(2,128)S(1)}, u32[]{:S(2)}, u32[]{:S(2)}) collective-permute-start(f32[4,2,256]{2,1,0:T(2,128)S(1)} %get-tuple-element.109), channel_id=1, source_target_pairs={{0,8},{8,16},{16,24},{1,9},{9,17},{17,25},{2,10},{10,18},{18,26},{... | collective-permute-start | bytes 24584 | tf_op jit(solution)/shard_map/ppermute | solution.py:20
  7.3 0.8 slice.30
  8.0 0.8 slice.31
  8.8 0.6 add_reduce_fusion
  9.4 0.7 convert_element_type.11
  10.8 0.0 collective-permute-done.7
  10.8 0.4 collective-permute-done.6
  11.2 132.2 %conditional.1 = (bf16[8,32,72,256]{3,2,1,0:T(8,128)(2,1)}, f32[4,384,256]{2,1,0:T(8,128)}) conditional(s32[]{:T(128)} %clamp.3, (s32[4,8]{1,0:T(4,128)}, f32[4,384,256]{2,1,0:T(8,128)}, f32[4,2,256]{2,1,0:T(2,128)S(1)}, f32[4,2,256]{2,1,0:T(2,128)S(1)}, f32[2,4]{1,0:T(2,128)S(1)}, /*index=5*/f32[8]{0:T(128)}, ...), branch_computations={%region_1.0_spmd, %region_2.0_spmd, %region_3.0_spmd} | conditional | flops 8 | bytes 41190392 | solution.py:393
  11.2 2.0 %branch_0_fun.5.sent = f32[4,4,104,256]{3,2,1,0:T(8,128)S(1)} custom-call(s32[4,8]{1,0:T(4,128)} %get-tuple-element.48.rows_ref, f32[4,384,256]{2,1,0:T(8,128)} %get-tuple-element.51.image_ref, f32[4,2,256]{2,1,0:T(2,128)S(1)} %get-tuple-element.52.above_ref, f32[4,2,256]{2,1,0:T(2,128)S(1)} %get-tuple-element.53.below_ref), custom_call_target="tpu_custom_call" | custom-call | tf_op jit(solution)/shard_map/cond/branch_0_fun/pallas_call | solution.py:55
  13.3 41.3 %branch_0_fun.6 = (f32[4,4,104,256]{3,2,1,0:T(8,128)S(1)}, f32[4,4,104,256]{3,2,1,0:T(8,128)S(1)}) custom-call(f32[4,4,104,256]{3,2,1,0:T(8,128)S(1)} %branch_0_fun.5.sent), custom_call_target="tpu_custom_call" | custom-call | tf_op jit(solution)/shard_map/cond/branch_0_fun/pallas_call | solution.py:163
  54.6 1.2 copy-done.10
  55.8 1.2 copy-done.11
  57.0 27.6 %branch_0_fun.7 = (bf16[8,32,72,256]{3,2,1,0:T(8,128)(2,1)}, f32[4,4,104,256]{3,2,1,0:T(8,128)}, f32[4,4,104,256]{3,2,1,0:T(8,128)}) custom-call(s32[4,8]{1,0:T(4,128)S(1)} %copy-done.12, f32[2,4]{1,0:T(2,128)S(1)} %get-tuple-element.49.low_ref, f32[8]{0:T(128)S(1)} %copy-done.15, f32[4,4,104,256]{3,2,1,0:T(8,128)} %copy-done.10, ...), custom_call_target="tpu_custom_call" | custom-call | tf_op jit(solution)/shard_map/cond/branch_0_fun/pallas_call | solution.py:342
  84.6 1.4 %copy-done.8 = f32[4,4,104,256]{3,2,1,0:T(8,128)S(1)} copy-done((f32[4,4,104,256]{3,2,1,0:T(8,128)S(1)}, f32[4,4,104,256]{3,2,1,0:T(8,128)}, u32[]{:S(2)}) %copy-start.8) | copy-done | bytes 1703960 | tf_op jit(solution)/shard_map/cond
  86.1 1.5 %copy-done.9 = f32[4,4,104,256]{3,2,1,0:T(8,128)S(1)} copy-done((f32[4,4,104,256]{3,2,1,0:T(8,128)S(1)}, f32[4,4,104,256]{3,2,1,0:T(8,128)}, u32[]{:S(2)}) %copy-start.9) | copy-done | bytes 1703960 | tf_op jit(solution)/shard_map/cond
  87.5 41.1 %branch_0_fun.8.windows_ref = f32[4,4,104,256]{3,2,1,0:T(8,128)S(1)} custom-call(f32[4,4,104,256]{3,2,1,0:T(8,128)S(1)} %copy-done.8, f32[4,4,104,256]{3,2,1,0:T(8,128)S(1)} %copy-done.9), custom_call_target="tpu_custom_call" | custom-call | tf_op jit(solution)/shard_map/cond/branch_0_fun/pallas_call | solution.py:208
  128.7 3.8 %collective-permute-start.1 = (f32[4,2,256]{2,1,0:T(2,128)S(1)}, f32[4,2,256]{2,1,0:T(2,128)S(1)}, u32[]{:S(2)}, u32[]{:S(2)}) collective-permute-start(f32[4,2,256]{2,1,0:T(2,128)S(1)} %slice_bitcast_fusion), channel_id=1, source_target_pairs={{8,0},{16,8},{24,16},{9,1},{17,9},{25,17},{10,2},{18,10},{26,18},{... | collective-permute-start | bytes 24584 | tf_op jit(solution)/shard_map/cond/branch_0_fun/ppermute | solution.py:20
  132.5 0.6 constant_dynamic-slice_fusion
  134.4 2.0 %collective-permute-start = (f32[4,2,256]{2,1,0:T(2,128)S(1)}, f32[4,2,256]{2,1,0:T(2,128)S(1)}, u32[]{:S(2)}, u32[]{:S(2)}) collective-permute-start(f32[4,2,256]{2,1,0:T(2,128)S(1)} %dynamic-slice_bitcast_fusion), channel_id=1, source_target_pairs={{0,8},{8,16},{16,24},{1,9},{9,17},{17,25},{2,10},{10,18},{18,26},{... | collective-permute-start | bytes 24584 | tf_op jit(solution)/shard_map/cond/branch_0_fun/ppermute | solution.py:20
  136.5 0.0 collective-permute-done.1.below_ref
  136.5 4.4 %collective-permute-done.above_ref = f32[4,2,256]{2,1,0:T(2,128)S(1)} collective-permute-done((f32[4,2,256]{2,1,0:T(2,128)S(1)}, f32[4,2,256]{2,1,0:T(2,128)S(1)}, u32[]{:S(2)}, u32[]{:S(2)}) %collective-permute-start) | collective-permute-done | bytes 8224 | tf_op jit(solution)/shard_map/cond/branch_0_fun/ppermute | solution.py:20
  140.9 2.5 %branch_0_fun.9 = f32[4,384,256]{2,1,0:T(8,128)} custom-call(s32[4,8]{1,0:T(4,128)S(1)} %copy-done.12, f32[4,4,104,256]{3,2,1,0:T(8,128)S(1)} %branch_0_fun.8.windows_ref, f32[4,2,256]{2,1,0:T(2,128)S(1)} %collective-permute-done.above_ref, f32[4,2,256]{2,1,0:T(2,128)S(1)} %collective-permute-done.1.below_ref), custom_call_target="tpu_custom_call" | custom-call | tf_op jit(solution)/shard_map/cond/branch_0_fun/pallas_call | solution.py:89
  (11 shorter events, 0.1 us)
Async XLA Ops:
  1.4 9.3 %collective-permute-start.7 = (f32[4,2,256]{2,1,0:T(2,128)S(1)}, f32[4,2,256]{2,1,0:T(2,128)S(1)}, u32[]{:S(2)}, u32[]{:S(2)}) collective-permute-start(f32[4,2,256]{2,1,0:T(2,128)S(1)} %get-tuple-element.108), channel_id=1, source_target_pairs={{8,0},{16,8},{24,16},{9,1},{17,9},{25,17},{10,2},{18,10},{26,18},{... | collective-permute-start | bytes 24584 | tf_op jit(solution)/shard_map/ppermute | solution.py:20
  4.8 6.4 %collective-permute-start.6 = (f32[4,2,256]{2,1,0:T(2,128)S(1)}, f32[4,2,256]{2,1,0:T(2,128)S(1)}, u32[]{:S(2)}, u32[]{:S(2)}) collective-permute-start(f32[4,2,256]{2,1,0:T(2,128)S(1)} %get-tuple-element.109), channel_id=1, source_target_pairs={{0,8},{8,16},{16,24},{1,9},{9,17},{17,25},{2,10},{10,18},{18,26},{... | collective-permute-start | bytes 24584 | tf_op jit(solution)/shard_map/ppermute | solution.py:20
  11.2 45.8 %copy-start.12 = (s32[4,8]{1,0:T(4,128)S(1)}, s32[4,8]{1,0:T(4,128)}, u32[]{:S(2)}) copy-start(s32[4,8]{1,0:T(4,128)} %get-tuple-element.48.rows_ref) | copy-start | bytes 388 | tf_op jit(solution)/shard_map/cond
  11.2 45.8 %copy-start.15 = (f32[8]{0:T(128)S(1)}, f32[8]{0:T(128)}, u32[]{:S(2)}) copy-start(f32[8]{0:T(128)} %get-tuple-element.96.thresholds_ref) | copy-start | bytes 100 | tf_op jit(solution)/shard_map/cond
  54.6 1.2 copy-start.10
  55.8 1.2 copy-start.11
  84.6 1.5 %copy-start.8 = (f32[4,4,104,256]{3,2,1,0:T(8,128)S(1)}, f32[4,4,104,256]{3,2,1,0:T(8,128)}, u32[]{:S(2)}) copy-start(f32[4,4,104,256]{3,2,1,0:T(8,128)} %get-tuple-element.58.own) | copy-start | bytes 5111812 | tf_op jit(solution)/shard_map/cond
  86.1 1.5 %copy-start.9 = (f32[4,4,104,256]{3,2,1,0:T(8,128)S(1)}, f32[4,4,104,256]{3,2,1,0:T(8,128)}, u32[]{:S(2)}) copy-start(f32[4,4,104,256]{3,2,1,0:T(8,128)} %get-tuple-element.59.other) | copy-start | bytes 5111812 | tf_op jit(solution)/shard_map/cond
  128.7 7.8 %collective-permute-start.1 = (f32[4,2,256]{2,1,0:T(2,128)S(1)}, f32[4,2,256]{2,1,0:T(2,128)S(1)}, u32[]{:S(2)}, u32[]{:S(2)}) collective-permute-start(f32[4,2,256]{2,1,0:T(2,128)S(1)} %slice_bitcast_fusion), channel_id=1, source_target_pairs={{8,0},{16,8},{24,16},{9,1},{17,9},{25,17},{10,2},{18,10},{26,18},{... | collective-permute-start | bytes 24584 | tf_op jit(solution)/shard_map/cond/branch_0_fun/ppermute | solution.py:20
  134.4 6.4 %collective-permute-start = (f32[4,2,256]{2,1,0:T(2,128)S(1)}, f32[4,2,256]{2,1,0:T(2,128)S(1)}, u32[]{:S(2)}, u32[]{:S(2)}) collective-permute-start(f32[4,2,256]{2,1,0:T(2,128)S(1)} %dynamic-slice_bitcast_fusion), channel_id=1, source_target_pairs={{0,8},{8,16},{16,24},{1,9},{9,17},{17,25},{2,10},{10,18},{18,26},{... | collective-permute-start | bytes 24584 | tf_op jit(solution)/shard_map/cond/branch_0_fun/ppermute | solution.py:20

commit v3 on v0

v3 whole, which is shorter than its diff:
```python
import functools

import jax
import jax.numpy as jnp
from jax import lax
from jax.experimental import pallas as pl
from jax.experimental.pallas import tpu as pltpu
from jax.sharding import PartitionSpec as P

HALO = 2
LEAD = 8
F32 = jnp.float32
BF16 = jnp.bfloat16
MESH = pl.DeviceIdType.MESH


def facet_starts(rows_ref):
    band = lax.axis_index("grp")
    starts = [jnp.int32(0)]
    for facet in range(rows_ref.shape[1]):
        starts.append(starts[-1] + rows_ref[band, facet])
    return starts


def position(chips):
    facet = lax.axis_index("fac")
    core = lax.rem(facet, 2)
    chip = lax.div(facet, 2)
    sibling = facet + 1 - 2 * core

    def at(r):
        return lax.rem(chip + r, chips)

    return core, chip, sibling, at


def remote(source, target, send, recv, device):
    return pltpu.make_async_remote_copy(
        src_ref=source, dst_ref=target, send_sem=send, recv_sem=recv,
        device_id=device, device_id_type=MESH,
    )


GROUP = 8


def tap(low_ref, d, a, k):
    count = low_ref.shape[1]
    high = low_ref[d, count - 1 - k] * (1.0 if k % 2 == 0 else -1.0)
    return jnp.where(a == 0, low_ref[d, k], high)


def moved(x, amount, way):
    amounts = jnp.full(x.shape, amount, jnp.int32)
    for bit in range(7):
        if 2**bit >= x.shape[0]:
            break
        turned = pltpu.roll(x, 2**bit if way > 0 else x.shape[0] - 2**bit, 0)
        x = jnp.where((amounts & 2**bit) != 0, turned, x)
    return x


def whole_kernel(
    cap, rows_ref, low_ref, thresholds_ref, cut_ref, image_ref, dual_ref,
    next_ref, windows, above_out, below_out,
    sent, own, other, arrived, stored, wide, strips, sums, terms, ahead, back,
    edge_above, edge_below, edge_spill,
    dual_sem, next_sem, edge_send, edge_recv,
    send, recv, pass_send, pass_recv, home_send, home_recv, sum_send, sum_recv,
):
    chips, share = sent.shape[:2]
    subbands, devices, _, capacity, columns = dual_ref.shape
    kinds = subbands // 2
    rows = image_ref.shape[1]
    flat = GROUP * capacity
    span = capacity + 8
    core, chip, sibling, at = position(chips)
    facet, band = lax.axis_index("fac"), lax.axis_index("grp")
    bands = lax.axis_size("grp")
    band_next, band_last = lax.rem(band + 1, bands), lax.rem(band + bands - 1, bands)

    def same_core(r):
        return {"fac": 2 * at(r) + core}

    def dual_load(c):
        return pltpu.make_async_copy(dual_ref.at[:, :, c], stored.at[c], dual_sem.at[c])

    def next_store(c):
        return pltpu.make_async_copy(stored.at[c], next_ref.at[:, :, c], next_sem.at[c])

    def remote_to(source, target, sends, recvs, r, c, device):
        return remote(source, target, sends.at[r, c], recvs.at[r, c], device)

    def outgoing(r, c):
        return remote_to(sent.at[at(r), c], own.at[chip, c], send, recv, r, c, same_core(r))

    def incoming(r, c):
        source = at(chips - r)
        return remote_to(sent.at[source, c], own.at[source, c], send, recv, r, c, same_core(r))

    def passing(r, c):
        source = at(chips - r)
        return remote_to(
            own.at[source, c], other.at[source, c], pass_send, pass_recv, r, c, {"fac": sibling}
        )

    def homing(r, c):
        return remote_to(
            other.at[at(r), c], arrived.at[at(r), c], home_send, home_recv, r, c,
            {"fac": sibling},
        )

    def returning(r, c):
        return remote_to(
            own.at[at(r), c], windows.at[chip, c], sum_send, sum_recv, r, c, same_core(r)
        )

    def returned(r, c):
        source = at(chips - r)
        return remote_to(
            own.at[source, c], windows.at[source, c], sum_send, sum_recv, r, c, same_core(r)
        )

    barrier = pltpu.get_barrier_semaphore()
    for device in [same_core(r) for r in range(1, chips)] + [
        {"fac": sibling}, {"grp": band_next}, {"grp": band_last},
    ]:
        pl.semaphore_signal(barrier, inc=1, device_id=device, device_id_type=MESH)
    pl.semaphore_wait(barrier, chips + 2)

    rims = [
        remote(image_ref.at[:, rows - 8 : rows], edge_above, edge_send.at[0], edge_recv.at[0],
               {"grp": band_next}),
        remote(image_ref.at[:, 0:8], edge_below, edge_send.at[1], edge_recv.at[1],
               {"grp": band_last}),
    ]
    for rim in rims:
        rim.start()

    into = lax.broadcasted_iota(jnp.int32, (columns, columns), 0)
    of = lax.broadcasted_iota(jnp.int32, (columns, columns), 1)

    def build(d, _):
        for b in range(2):
            forward = jnp.zeros((columns, columns), F32)
            adjoint = jnp.zeros((columns, columns), F32)
            for k in range(2 * HALO):
                value = tap(low_ref, d, b, k)
                forward = jnp.where(into - of + HALO == k, value, forward)
                adjoint = jnp.where(of - into + HALO == k, value, adjoint)
            forward = forward.astype(BF16)
            ahead[d, 0:columns, b * columns : (b + 1) * columns] = forward
            ahead[d, columns : 2 * columns, b * columns : (b + 1) * columns] = forward
            back[d, b * columns : (b + 1) * columns, :] = adjoint.astype(BF16)
        return 0

    starts = facet_starts(rows_ref)
    last_rows = starts[2 * chips] - starts[2 * chips - 2]
    for rim in rims:
        rim.wait()
    row = lax.broadcasted_iota(jnp.int32, (cap, columns), 0)

    def rimmed(pair, c):
        window = cut_ref[pair, c]
        fill = jnp.zeros((cap - HALO, columns), F32)
        above = jnp.concatenate([edge_above[c, 8 - HALO : 8, :], fill], 0)
        first = (row < HALO) & (pair == 0) & (band > 0)
        window = jnp.where(first, above, window)
        for i in range(HALO - 1):
            below = jnp.broadcast_to(edge_below[c, i : i + 1, :], (cap, columns))
            last = (row == HALO + last_rows + i) & (pair == chips - 1) & (band < bands - 1)
            window = jnp.where(last, below, window)
        return window

    def cut(c, _):
        for r in list(range(1, chips)) + [0]:
            if r:
                sent[at(r), c] = rimmed(at(r), c)
                outgoing(r, c).start()
            else:
                own[chip, c] = rimmed(chip, c)
                passing(0, c).start()
        return 0

    lax.fori_loop(0, share, cut, 0)
    for c in range(share):
        dual_load(c).start()
    lax.fori_loop(0, low_ref.shape[0], build, 0)
    sums[...] = jnp.zeros_like(sums)

    offset = jnp.where(core == 0, 0, rows_ref[band, facet - core])
    length = rows_ref[band, facet]
    keep = lax.broadcasted_iota(jnp.int32, (capacity, columns), 0) < length

    def analyse(c, _):
        for r in range(1, chips):
            incoming(r, c).wait_recv()
            passing(r, c).start()
        for r in range(chips):
            passing(r, c).wait_recv()
        dual_load(c).wait()
        for g in range(devices // GROUP):
            for source, half in ((own, core), (other, 1 - core)):
                for j in range(GROUP // 2):
                    window = source[g * (GROUP // 2) + j, c]
                    strips[2 * j + half] = moved(window, offset, -1)[:span]

            def one_kind(step, _):
                d, a = step // 2, step % 2
                sent_rows = tap(low_ref, d, a, 0) * strips[:, 0:capacity, :]
                for k in range(1, 2 * HALO):
                    sent_rows += tap(low_ref, d, a, k) * strips[:, k : k + capacity, :]
                flat_rows = sent_rows.reshape(flat, columns)
                high = flat_rows.astype(BF16)
                low = (flat_rows - high.astype(F32)).astype(BF16)
                both = jnp.concatenate([high, low], axis=1)
                coefficient = jnp.dot(both, ahead[d], preferred_element_type=F32)
                for b in range(2):
                    part = coefficient[:, b * columns : (b + 1) * columns]
                    part = part.reshape(GROUP, capacity, columns)
                    here = pl.ds(g * GROUP, GROUP)
                    u = stored[c, 2 * step + b, here].astype(F32) + part
                    u = jnp.where(keep, u, 0.0)
                    wide[c, 2 * step + b, here] = u
                    sums[2 * step + b] += jnp.sum(u * u, axis=0)
                return 0

            lax.fori_loop(0, kinds, one_kind, 0)
        return 0

    lax.fori_loop(0, share, analyse, 0)

    def scale(s, _):
        radius = thresholds_ref[s]
        sums[s] = radius / jnp.maximum(jnp.sqrt(sums[s]), radius)
        return 0

    lax.fori_loop(0, subbands, scale, 0)

    def settle(c, _):
        for r in range(chips):
            passing(r, c).wait_send()
            if r:
                outgoing(r, c).wait_send()
        return 0

    lax.fori_loop(0, share, settle, 0)

    def synthesise(c, _):
        for g in range(devices // GROUP):
            here = pl.ds(g * GROUP, GROUP)

            def one_kind(step, _):
                parts = []
                for b in range(2):
                    scaled = (wide[c, 2 * step + b, here] * sums[2 * step + b]).astype(BF16)
                    stored[c, 2 * step + b, here] = scaled
                    parts.append(scaled.reshape(flat, columns))
                both = jnp.concatenate(parts, axis=1)
                term = jnp.dot(both, back[step // 2], preferred_element_type=F32)
                terms[step] = term.reshape(GROUP, capacity, columns)
                return 0

            lax.fori_loop(0, kinds, one_kind, 0)
            for target, half in ((own, core), (other, 1 - core)):
                def place(j, _, target=target, half=half):
                    loaded = [terms[step, 2 * j + half] for step in range(kinds)]
                    merged = jnp.zeros((span, columns), F32)
                    for k in range(2 * HALO):
                        tap_sum = tap(low_ref, 0, 0, k) * loaded[0]
                        for step in range(1, kinds):
                            tap_sum += tap(low_ref, step // 2, step % 2, k) * loaded[step]
                        spare = jnp.zeros((span - capacity, columns), F32)
                        tall = jnp.concatenate([tap_sum, spare], 0)
                        merged += pltpu.roll(tall, k, 0) if k else tall
                    merged = jnp.concatenate([merged, jnp.zeros((cap - span, columns), F32)], 0)
                    target[g * (GROUP // 2) + j, c] = moved(merged, offset, 1)
                    return 0

                lax.fori_loop(0, GROUP // 2, place, 0)
        for r in list(range(1, chips)) + [0]:
            homing(r, c).start()
        next_store(c).start()
        for r in list(range(1, chips)) + [0]:
            homing(r, c).wait_recv()
            if r:
                own[at(r), c] = own[at(r), c] + arrived[at(r), c]
                returning(r, c).start()
            else:
                windows[chip, c] = own[chip, c] + arrived[chip, c]
        return 0

    lax.fori_loop(0, share, synthesise, 0)

    def finish(c, _):
        for r in range(chips):
            homing(r, c).wait_send()
            if r:
                returned(r, c).wait_recv()
                returning(r, c).wait_send()
        next_store(c).wait()
        return 0

    lax.fori_loop(0, share, finish, 0)

    for c in range(share):
        edge_spill[c] = jnp.zeros((8, columns), F32)
        for i in range(HALO - 1):
            found = jnp.where(row == HALO + last_rows + i, windows[chips - 1, c], 0.0)
            edge_spill[c, i : i + 1, :] = jnp.sum(found, axis=0, keepdims=True)
    spills = [
        remote(edge_spill, above_out, edge_send.at[2], edge_recv.at[2], {"grp": band_next}),
        remote(windows.at[0, :, 0:8], below_out, edge_send.at[3], edge_recv.at[3],
               {"grp": band_last}),
    ]
    for spill in spills:
        spill.start()
    for spill in spills:
        spill.wait()


def whole(facet_rows, lows, thresholds, pieces, image, dual, cap, collective_id):
    subbands, devices, share, capacity, columns = dual.shape
    chips, kinds = devices // 2, subbands // 2
    smem = pl.BlockSpec(memory_space=pltpu.SMEM)
    vmem = pl.BlockSpec(memory_space=pltpu.VMEM)
    free = pl.BlockSpec(memory_space=pl.ANY)
    windows = (chips, share, cap, columns)
    rim = jax.ShapeDtypeStruct((share, 8, columns), F32)
    dma = pltpu.SemaphoreType.DMA
    return pl.pallas_call(
        functools.partial(whole_kernel, cap),
        out_shape=(
            jax.ShapeDtypeStruct(dual.shape, dual.dtype), jax.ShapeDtypeStruct(windows, F32),
            rim, rim,
        ),
        in_specs=[smem, smem, smem, vmem, free, free],
        out_specs=(free, vmem, vmem, vmem),
        scratch_shapes=[
            *[pltpu.VMEM(windows, F32)] * 4,
            pltpu.VMEM((share, subbands, devices, capacity, columns), BF16),
            pltpu.VMEM((share, subbands, devices, capacity, columns), F32),
            pltpu.VMEM((GROUP, capacity + 8, columns), F32),
            pltpu.VMEM((subbands, capacity, columns), F32),
            pltpu.VMEM((kinds, GROUP, capacity, columns), F32),
            pltpu.VMEM((kinds // 2, 2 * columns, 2 * columns), BF16),
            pltpu.VMEM((kinds // 2, 2 * columns, columns), BF16),
            *[pltpu.VMEM((share, 8, columns), F32)] * 3,
            dma((share,)), dma((share,)), dma((4,)), dma((4,)),
            *[dma((chips, share))] * 8,
        ],
        compiler_params=pltpu.CompilerParams(
            collective_id=collective_id, has_side_effects=True, vmem_limit_bytes=62 * 2**20
        ),
    )(facet_rows, lows, thresholds, pieces, image, dual)


def cut_kernel(cap, rows_ref, image_ref, out_ref, padded):
    rows = image_ref.shape[1]
    share, _, columns = padded.shape
    padded[:, 0:LEAD, :] = jnp.zeros((share, LEAD, columns), F32)
    tail = padded.shape[1] - LEAD - rows
    padded[:, LEAD + rows :, :] = jnp.zeros((share, tail, columns), F32)
    padded[:, LEAD : LEAD + rows, :] = image_ref[...]
    starts = facet_starts(rows_ref)

    for pair in range(out_ref.shape[0]):
        begin = starts[2 * pair] + (LEAD - HALO)
        base = pl.multiple_of((begin // 8) * 8, 8)
        turn = cap + 8 - (begin - base)

        @pl.loop(0, out_ref.shape[1])
        def _(channel):
            window = padded[channel, pl.ds(base, cap + 8), :]
            out_ref[pair, channel] = pltpu.roll(window, turn, 0)[:cap]


def cut(facet_rows, image, pairs, cap):
    channels, rows, columns = image.shape
    vmem = pl.BlockSpec(memory_space=pltpu.VMEM)
    return pl.pallas_call(
        functools.partial(cut_kernel, cap),
        out_shape=jax.ShapeDtypeStruct((pairs, channels, cap, columns), F32),
        in_specs=[pl.BlockSpec(memory_space=pltpu.SMEM), vmem],
        out_specs=vmem,
        scratch_shapes=[pltpu.VMEM((channels, LEAD + rows + cap + 16, columns), F32)],
        compiler_params=pltpu.CompilerParams(vmem_limit_bytes=48 * 2**20),
    )(facet_rows, image)


def join_kernel(
    cap, rows_ref, windows_ref, above_ref, below_ref, made_ref, out_ref, next_ref, padded, sems
):
    rows = out_ref.shape[1]
    moves = [
        pltpu.make_async_copy(made_ref.at[s], next_ref.at[s], sems.at[s])
        for s in range(made_ref.shape[0])
    ]
    for move in moves:
        move.start()
    padded[...] = jnp.zeros_like(padded)
    starts = facet_starts(rows_ref)
    band, bands = lax.axis_index("grp"), lax.axis_size("grp")

    for pair in range(windows_ref.shape[0]):
        begin = starts[2 * pair] + (LEAD - HALO)
        base = pl.multiple_of((begin // 8) * 8, 8)

        @pl.loop(0, windows_ref.shape[1])
        def _(channel):
            window = windows_ref[pair, channel]
            window = jnp.concatenate([window, jnp.zeros((8, window.shape[1]), F32)], 0)
            here = (channel, pl.ds(base, cap + 8), slice(None))
            padded[here] = padded[here] + pltpu.roll(window, begin - base, 0)

    out_ref[...] = padded[:, LEAD : LEAD + rows, :]
    above = jnp.where(band > 0, above_ref[:, 0:HALO, :], 0.0)
    below = jnp.where(band < bands - 1, below_ref[:, 0:HALO, :], 0.0)
    out_ref[:, 0:HALO, :] = out_ref[:, 0:HALO, :] + above
    out_ref[:, rows - HALO : rows, :] = out_ref[:, rows - HALO : rows, :] + below
    for move in moves:
        move.wait()


def join(facet_rows, windows, above, below, made, rows):
    pairs, channels, cap, columns = windows.shape
    vmem = pl.BlockSpec(memory_space=pltpu.VMEM)
    free = pl.BlockSpec(memory_space=pl.ANY)
    return pl.pallas_call(
        functools.partial(join_kernel, cap),
        out_shape=(
            jax.ShapeDtypeStruct((channels, rows, columns), F32),
            jax.ShapeDtypeStruct(made.shape, made.dtype),
        ),
        in_specs=[pl.BlockSpec(memory_space=pltpu.SMEM), vmem, vmem, vmem, free],
        out_specs=(vmem, free),
        scratch_shapes=[
            pltpu.VMEM((channels, LEAD + rows + cap + 16, columns), F32),
            pltpu.SemaphoreType.DMA((made.shape[0],)),
        ],
        compiler_params=pltpu.CompilerParams(vmem_limit_bytes=48 * 2**20),
    )(facet_rows, windows, above, below, made)


def on_device(image_cube, dual, lowpass, thresholds, facet_rows):
    groups = lax.axis_size("fac")
    share, band_rows, _ = image_cube.shape
    subbands, _, capacity, columns = dual.shape
    lows = lowpass.astype(F32)
    by_device = dual.reshape(subbands, groups, share, capacity, columns)

    def run(choice, cap):
        def body():
            pieces = cut(facet_rows, image_cube, groups // 2, cap)
            made, windows, above, below = whole(
                facet_rows, lows, thresholds, pieces, image_cube, by_device, cap, choice
            )
            prior_term, updated = join(facet_rows, windows, above, below, made, band_rows)
            return updated.reshape(dual.shape), prior_term

        return body

    most = jnp.max(facet_rows[:, ::2] + facet_rows[:, 1::2]) + 2 * HALO
    mean = 2 * band_rows // groups
    steps = [mean, (mean + 2 * capacity) // 2, 2 * capacity]
    caps = [-(-(rows + 2 * HALO) // 8) * 8 for rows in steps]
    choice = (most > caps[0]).astype(jnp.int32) + (most > caps[1]).astype(jnp.int32)
    return lax.switch(choice, [run(i, cap) for i, cap in enumerate(caps)])


def solution(mesh):
    placed = (P("fac", "grp", None), P(None, None, ("grp", "fac"), None), P(), P(), P())
    return jax.shard_map(
        on_device,
        mesh=mesh,
        in_specs=placed,
        out_specs=(P(None, None, ("grp", "fac"), None), P("fac", "grp", None)),
        check_vma=False,
    )
```

time: 306 us -> 398 us (1.30)
  Pallas kernels: 0 us -> 387 us
  other arithmetic: 160 us -> 1.29 us
  waiting for transfers between devices: 83 us -> 0 us
  starting transfers between devices: 28.1 us -> 0 us
  local copies, waits for them, and re-layouts: 28.2 us -> 5.7 us
    pallas_call x0 -> x3, Pallas kernels: none -> 387 us  [the longest x1 289 us: join(): pl.pallas_call(functools.partial(join_kernel, cap), out_shape=(jax.ShapeD...]
    add x7 -> x0, other arithmetic: 85.7 us -> none  [the longest x1 34.3 us: on_device(): merged + column_adjoint(row_sums[column_kind], filter_pair[column_kind])]
    all_to_all x2 -> x0, waiting for transfers between devices: 81.2 us -> none  [the longest x1 48.6 us: on_device(): lax.all_to_all(picked, 'fac', split_axis=1, concat_axis=0, tiled=True)]
    reduce_sum x5 -> x0, other arithmetic: 37 us -> none  [the longest x4 36.9 us: on_device(): magnitude = jnp.sqrt(jnp.sum(combined * combined, axis=0))]
    ppermute x4 -> x0, starting transfers between devices: 18.5 us -> none  [shifted(): return lax.ppermute(x, axis, pairs)]
    gather x3 -> x0, local copies, waits for them, and re-layouts: 10.4 us -> none  [the longest x1 6.55 us: on_device(): picked = jnp.take(image_cube, jnp.clip(row_index, 0, band_rows - 1), axis=1)]
    unnamed x7 -> x0, other arithmetic: 10.3 us -> none
    all_to_all x2 -> x0, starting transfers between devices: 9.64 us -> none  [the longest x1 5.01 us: on_device(): lax.all_to_all(picked, 'fac', split_axis=1, concat_axis=0, tiled=True)]
  transfers between devices with their start and end apart: 6 -> 0, of which waited for: 3 -> 0; matrix products, arithmetic and copies ran while one was open for 9% -> 0% of each run, Pallas kernels for 0% -> 0%
where the time goes in v3:
time: 398 us; the launch traced here: 395 us
  Pallas kernels  387 us (97%)
  local copies, waits for them, and re-layouts  5.7 us (1%)
    pallas_call x1, Pallas kernels, join(): pl.pallas_call(functools.partial(join_kernel, cap), out_shape=(jax.ShapeD...  289 us
    pallas_call x1, Pallas kernels, whole(): pl.pallas_call(functools.partial(whole_kernel, cap), out_shape=(jax.Shape...  96.1 us

profile of v3, /device:TPU:4, one launch (start us, length us, event | category | flops | bytes accessed | tf_op | source)
XLA Modules:
  0.0 395.4 jit_solution(9742374837634213946)
XLA Ops:
  0.6 0.7 convert_element_type.11
  1.3 0.8 slice.6
  2.1 0.8 slice.7
  2.8 0.6 add_reduce_fusion
  4.1 391.3 %conditional.1 = (f32[4,384,256]{2,1,0:T(8,128)}, bf16[8,32,72,256]{3,2,1,0:T(8,128)(2,1)}) conditional(s32[]{:T(128)} %clamp.3, (s32[4,8]{1,0:T(4,128)}, f32[4,384,256]{2,1,0:T(8,128)}, f32[2,4]{1,0:T(2,128)S(1)}, f32[8]{0:T(128)}, bf16[8,32,72,256]{3,2,1,0:T(8,128)(2,1)}) %tuple.19, (s32[4,8]{1,0:T(4,128)}, ...), branch_computations={%region_1.0_spmd, %region_2.0_spmd, %region_3.0_spmd} | conditional | bytes 26477396 | solution.py:468
  4.1 0.0 copy-start.12
  4.1 0.0 copy-start.15
  4.2 0.0 copy-start.18
  4.2 2.1 branch_0_fun.3.cut_ref
  6.3 0.0 copy-start.2
  6.3 1.2 copy-done.2
  7.5 0.0 copy-done.12
  7.5 0.0 copy-done.15
  7.5 0.0 copy-done.18
  7.5 96.1 %branch_0_fun.4 = (bf16[8,8,4,72,256]{4,3,2,1,0:T(8,128)(2,1)}, f32[4,4,104,256]{3,2,1,0:T(8,128)}, f32[4,8,256]{2,1,0:T(8,128)}, f32[4,8,256]{2,1,0:T(8,128)}) custom-call(s32[4,8]{1,0:T(4,128)S(1)} %copy-done.15, f32[2,4]{1,0:T(2,128)S(1)} %get-tuple-element.31.low_ref, f32[8]{0:T(128)S(1)} %copy-done.18, f32[4,4,104,256]{3,2,1,0:T(8,128)} %copy-done.2, ...), custom_call_target="tpu_custom_call" | custom-call | tf_op jit(solution)/shard_map/cond/branch_0_fun/pallas_call | solution.py:331
  103.6 0.0 copy-start.5
  103.7 1.4 copy-done.5
  105.1 0.0 copy-start.6
  105.1 0.8 copy-done.6
  105.9 0.0 copy-start.7
  105.9 0.8 copy-done.7
  106.6 288.8 %branch_0_fun.5 = (f32[4,384,256]{2,1,0:T(8,128)}, bf16[8,8,4,72,256]{4,3,2,1,0:T(8,128)(2,1)}) custom-call(s32[4,8]{1,0:T(4,128)S(1)} %copy-done.15, f32[4,4,104,256]{3,2,1,0:T(8,128)S(1)} %copy-done.5, f32[4,8,256]{2,1,0:T(8,128)S(1)} %copy-done.6, f32[4,8,256]{2,1,0:T(8,128)S(1)} %copy-done.7, bf16[8,8,4,72,256]{4,3,2,1,0:T(8,128)(2,1)} %get-tuple-element.38.made_ref), custom_call_target="tpu_custom_call" | custom-call | tf_op jit(solution)/shard_map/cond/branch_0_fun/pallas_call | solution.py:429
Async XLA Ops:
  4.1 3.4 copy-start.12
  4.1 3.4 copy-start.15
  4.2 3.3 copy-start.18
  6.3 1.2 copy-start.2
  103.6 1.5 copy-start.5
  105.1 0.8 copy-start.6
  105.9 0.8 copy-start.7

commit v4 on v3

--- a/solution.py
+++ b/solution.py
@@ -23,13 +23,18 @@
 
 
 def position(chips):
+    assert chips & (chips - 1) == 0
     facet = lax.axis_index("fac")
     core = lax.rem(facet, 2)
     chip = lax.div(facet, 2)
     sibling = facet + 1 - 2 * core
 
     def at(r):
-        return lax.rem(chip + r, chips)
+        other = chip
+        for bit in range(chips.bit_length() - 1):
+            if r & 2**bit:
+                other = other + 2**bit * (1 - 2 * lax.rem(lax.div(chip, 2**bit), 2))
+        return other
 
     return core, chip, sibling, at
 
@@ -95,11 +100,11 @@
         return remote_to(sent.at[at(r), c], own.at[chip, c], send, recv, r, c, same_core(r))
 
     def incoming(r, c):
-        source = at(chips - r)
+        source = at(r)
         return remote_to(sent.at[source, c], own.at[source, c], send, recv, r, c, same_core(r))
 
     def passing(r, c):
-        source = at(chips - r)
+        source = at(r)
         return remote_to(
             own.at[source, c], other.at[source, c], pass_send, pass_recv, r, c, {"fac": sibling}
         )
@@ -116,7 +121,7 @@
         )
 
     def returned(r, c):
-        source = at(chips - r)
+        source = at(r)
         return remote_to(
             own.at[source, c], windows.at[source, c], sum_send, sum_recv, r, c, same_core(r)
         )
@@ -173,7 +178,7 @@
         return window
 
     def cut(c, _):
-        for r in list(range(1, chips)) + [0]:
+        for r in list(range(chips - 1, -1, -1)):
             if r:
                 sent[at(r), c] = rimmed(at(r), c)
                 outgoing(r, c).start()
@@ -193,7 +198,7 @@
     keep = lax.broadcasted_iota(jnp.int32, (capacity, columns), 0) < length
 
     def analyse(c, _):
-        for r in range(1, chips):
+        for r in range(chips - 1, 0, -1):
             incoming(r, c).wait_recv()
             passing(r, c).start()
         for r in range(chips):
@@ -278,10 +283,10 @@
                     return 0
 
                 lax.fori_loop(0, GROUP // 2, place, 0)
-        for r in list(range(1, chips)) + [0]:
+        for r in list(range(chips - 1, -1, -1)):
             homing(r, c).start()
         next_store(c).start()
-        for r in list(range(1, chips)) + [0]:
+        for r in list(range(chips - 1, -1, -1)):
             homing(r, c).wait_recv()
             if r:
                 own[at(r), c] = own[at(r), c] + arrived[at(r), c]
@@ -389,15 +394,21 @@
 
 
 def join_kernel(
-    cap, rows_ref, windows_ref, above_ref, below_ref, made_ref, out_ref, next_ref, padded, sems
+    cap, rows_ref, windows_ref, above_ref, below_ref, made_ref, out_ref, next_ref,
+    padded, staged, load_sems, store_sems,
 ):
     rows = out_ref.shape[1]
-    moves = [
-        pltpu.make_async_copy(made_ref.at[s], next_ref.at[s], sems.at[s])
-        for s in range(made_ref.shape[0])
+    subbands = made_ref.shape[0]
+    loads = [
+        pltpu.make_async_copy(made_ref.at[s], staged.at[s], load_sems.at[s])
+        for s in range(subbands)
     ]
-    for move in moves:
-        move.start()
+    stores = [
+        pltpu.make_async_copy(staged.at[s], next_ref.at[s], store_sems.at[s])
+        for s in range(subbands)
+    ]
+    for load in loads:
+        load.start()
     padded[...] = jnp.zeros_like(padded)
     starts = facet_starts(rows_ref)
     band, bands = lax.axis_index("grp"), lax.axis_size("grp")
@@ -413,13 +424,18 @@
             here = (channel, pl.ds(base, cap + 8), slice(None))
             padded[here] = padded[here] + pltpu.roll(window, begin - base, 0)
 
+        pairs = windows_ref.shape[0]
+        for s in range(pair * subbands // pairs, (pair + 1) * subbands // pairs):
+            loads[s].wait()
+            stores[s].start()
+
     out_ref[...] = padded[:, LEAD : LEAD + rows, :]
     above = jnp.where(band > 0, above_ref[:, 0:HALO, :], 0.0)
     below = jnp.where(band < bands - 1, below_ref[:, 0:HALO, :], 0.0)
     out_ref[:, 0:HALO, :] = out_ref[:, 0:HALO, :] + above
     out_ref[:, rows - HALO : rows, :] = out_ref[:, rows - HALO : rows, :] + below
-    for move in moves:
-        move.wait()
+    for store in stores:
+        store.wait()
 
 
 def join(facet_rows, windows, above, below, made, rows):
@@ -436,6 +452,8 @@
         out_specs=(vmem, free),
         scratch_shapes=[
             pltpu.VMEM((channels, LEAD + rows + cap + 16, columns), F32),
+            pltpu.VMEM(made.shape, made.dtype),
+            pltpu.SemaphoreType.DMA((made.shape[0],)),
             pltpu.SemaphoreType.DMA((made.shape[0],)),
         ],
         compiler_params=pltpu.CompilerParams(vmem_limit_bytes=48 * 2**20),
@@ -460,7 +478,7 @@
 
         return body
 
-    most = jnp.max(facet_rows[:, ::2] + facet_rows[:, 1::2]) + 2 * HALO
+    most = jnp.max(jnp.sum(facet_rows.reshape(-1, 2), axis=1)) + 2 * HALO
     mean = 2 * band_rows // groups
     steps = [mean, (mean + 2 * capacity) // 2, 2 * capacity]
     caps = [-(-(rows + 2 * HALO) // 8) * 8 for rows in steps]

time: 398 us -> 119 us (0.30)
  Pallas kernels: 387 us -> 109 us
    pallas_call x1, Pallas kernels: 289 us -> 9.06 us  [join(): pl.pallas_call(functools.partial(join_kernel, cap), out_shape=(jax.ShapeD...]
where the time goes in v4:
time: 119 us; the launch traced here: 116 us
  Pallas kernels  109 us (92%)
  local copies, waits for them, and re-layouts  4.92 us (4%)
  other arithmetic  1.41 us (1%)
  between operations  1.29 us (1%)
    pallas_call x1, Pallas kernels, whole(): pl.pallas_call(functools.partial(whole_kernel, cap), out_shape=(jax.Shape...  97.6 us
    pallas_call x1, Pallas kernels, join(): pl.pallas_call(functools.partial(join_kernel, cap), out_shape=(jax.ShapeD...  9.06 us
    cond x14, local copies, waits for them, and re-layouts  4.16 us

profile of v4, /device:TPU:4, one launch (start us, length us, event | category | flops | bytes accessed | tf_op | source)
XLA Modules:
  0.0 116.5 jit_solution(2801683943732124392)
XLA Ops:
  0.6 0.7 convert_element_type.11
  1.3 0.8 reshape.19
  2.0 0.1 reduce_sum.9
  2.2 0.6 reduce_max.9
  3.5 113.0 %conditional.1 = (f32[4,384,256]{2,1,0:T(8,128)}, bf16[8,32,72,256]{3,2,1,0:T(8,128)(2,1)}) conditional(s32[]{:T(128)} %clamp.3, (s32[4,8]{1,0:T(4,128)}, f32[4,384,256]{2,1,0:T(8,128)}, f32[2,4]{1,0:T(2,128)S(1)}, f32[8]{0:T(128)}, bf16[8,32,72,256]{3,2,1,0:T(8,128)(2,1)}) %tuple.19, (s32[4,8]{1,0:T(4,128)}, ...), branch_computations={%region_2.0_spmd, %region_3.0_spmd, %region_4.0_spmd} | conditional | bytes 26477396 | solution.py:486
  3.5 0.0 copy-start.12
  3.5 0.0 copy-start.15
  3.5 0.0 copy-start.18
  3.5 2.1 %branch_0_fun.3.cut_ref = f32[4,4,104,256]{3,2,1,0:T(8,128)S(1)} custom-call(s32[4,8]{1,0:T(4,128)} %get-tuple-element.30.rows_ref, f32[4,384,256]{2,1,0:T(8,128)} %get-tuple-element.75.image_ref), custom_call_target="tpu_custom_call" | custom-call | tf_op jit(solution)/shard_map/cond/branch_0_fun/pallas_call | solution.py:386
  5.6 0.0 copy-start.2
  5.7 1.2 %copy-done.2 = f32[4,4,104,256]{3,2,1,0:T(8,128)} copy-done((f32[4,4,104,256]{3,2,1,0:T(8,128)}, f32[4,4,104,256]{3,2,1,0:T(8,128)S(1)}, u32[]{:S(2)}) %copy-start.2) | copy-done | bytes 1703960 | tf_op jit(solution)/shard_map/cond
  6.8 0.0 copy-done.12
  6.8 0.0 copy-done.15
  6.8 0.0 copy-done.18
  6.8 97.6 %branch_0_fun.4 = (bf16[8,8,4,72,256]{4,3,2,1,0:T(8,128)(2,1)}, f32[4,4,104,256]{3,2,1,0:T(8,128)}, f32[4,8,256]{2,1,0:T(8,128)}, f32[4,8,256]{2,1,0:T(8,128)}) custom-call(s32[4,8]{1,0:T(4,128)S(1)} %copy-done.15, f32[2,4]{1,0:T(2,128)S(1)} %get-tuple-element.31.low_ref, f32[8]{0:T(128)S(1)} %copy-done.18, f32[4,4,104,256]{3,2,1,0:T(8,128)} %copy-done.2, ...), custom_call_target="tpu_custom_call" | custom-call | tf_op jit(solution)/shard_map/cond/branch_0_fun/pallas_call | solution.py:336
  104.4 0.0 copy-start.5
  104.4 1.4 %copy-done.5 = f32[4,4,104,256]{3,2,1,0:T(8,128)S(1)} copy-done((f32[4,4,104,256]{3,2,1,0:T(8,128)S(1)}, f32[4,4,104,256]{3,2,1,0:T(8,128)}, u32[]{:S(2)}) %copy-start.5) | copy-done | bytes 1703960 | tf_op jit(solution)/shard_map/cond
  105.9 0.0 copy-start.6
  105.9 0.8 copy-done.6
  106.6 0.0 copy-start.7
  106.6 0.8 copy-done.7
  107.4 9.1 %branch_0_fun.5 = (f32[4,384,256]{2,1,0:T(8,128)}, bf16[8,8,4,72,256]{4,3,2,1,0:T(8,128)(2,1)}) custom-call(s32[4,8]{1,0:T(4,128)S(1)} %copy-done.15, f32[4,4,104,256]{3,2,1,0:T(8,128)S(1)} %copy-done.5, f32[4,8,256]{2,1,0:T(8,128)S(1)} %copy-done.6, f32[4,8,256]{2,1,0:T(8,128)S(1)} %copy-done.7, bf16[8,8,4,72,256]{4,3,2,1,0:T(8,128)(2,1)} %get-tuple-element.38.made_ref), custom_call_target="tpu_custom_call" | custom-call | tf_op jit(solution)/shard_map/cond/branch_0_fun/pallas_call | solution.py:445
Async XLA Ops:
  3.5 3.4 %copy-start.12 = (f32[4,384,256]{2,1,0:T(8,128)S(1)}, f32[4,384,256]{2,1,0:T(8,128)}, u32[]{:S(2)}) copy-start(f32[4,384,256]{2,1,0:T(8,128)} %get-tuple-element.75.image_ref) | copy-start | bytes 4718596 | tf_op jit(solution)/shard_map/cond
  3.5 3.4 %copy-start.15 = (s32[4,8]{1,0:T(4,128)S(1)}, s32[4,8]{1,0:T(4,128)}, u32[]{:S(2)}) copy-start(s32[4,8]{1,0:T(4,128)} %get-tuple-element.30.rows_ref) | copy-start | bytes 388 | tf_op jit(solution)/shard_map/cond
  3.5 3.3 %copy-start.18 = (f32[8]{0:T(128)S(1)}, f32[8]{0:T(128)}, u32[]{:S(2)}) copy-start(f32[8]{0:T(128)} %get-tuple-element.78.thresholds_ref) | copy-start | bytes 100 | tf_op jit(solution)/shard_map/cond
  5.6 1.2 %copy-start.2 = (f32[4,4,104,256]{3,2,1,0:T(8,128)}, f32[4,4,104,256]{3,2,1,0:T(8,128)S(1)}, u32[]{:S(2)}) copy-start(f32[4,4,104,256]{3,2,1,0:T(8,128)S(1)} %branch_0_fun.3.cut_ref) | copy-start | bytes 5111812 | tf_op jit(solution)/shard_map/cond
  104.4 1.5 %copy-start.5 = (f32[4,4,104,256]{3,2,1,0:T(8,128)S(1)}, f32[4,4,104,256]{3,2,1,0:T(8,128)}, u32[]{:S(2)}) copy-start(f32[4,4,104,256]{3,2,1,0:T(8,128)} %get-tuple-element.35.windows_ref) | copy-start | bytes 5111812 | tf_op jit(solution)/shard_map/cond
  105.9 0.8 copy-start.6
  106.6 0.8 copy-start.7

commit v5 on v4

--- a/solution.py
+++ b/solution.py
@@ -70,7 +70,7 @@
     next_ref, windows, above_out, below_out,
     sent, own, other, arrived, stored, wide, strips, sums, terms, ahead, back,
     edge_above, edge_below, edge_spill,
-    dual_sem, next_sem, edge_send, edge_recv,
+    cut_sem, dual_sem, next_sem, edge_send, edge_recv,
     send, recv, pass_send, pass_recv, home_send, home_recv, sum_send, sum_recv,
 ):
     chips, share = sent.shape[:2]
@@ -126,6 +126,8 @@
             own.at[source, c], windows.at[source, c], sum_send, sum_recv, r, c, same_core(r)
         )
 
+    cut_load = pltpu.make_async_copy(cut_ref, sent, cut_sem)
+    cut_load.start()
     barrier = pltpu.get_barrier_semaphore()
     for device in [same_core(r) for r in range(1, chips)] + [
         {"fac": sibling}, {"grp": band_next}, {"grp": band_last},
@@ -161,12 +163,18 @@
 
     starts = facet_starts(rows_ref)
     last_rows = starts[2 * chips] - starts[2 * chips - 2]
+    cut_load.wait()
+    inner = [(at(r) > 0) & (at(r) < chips - 1) for r in range(chips)]
+    for r in range(chips - 1, 0, -1):
+        @pl.when(inner[r])
+        def _(r=r):
+            outgoing(r, 0).start()
     for rim in rims:
         rim.wait()
     row = lax.broadcasted_iota(jnp.int32, (cap, columns), 0)
 
     def rimmed(pair, c):
-        window = cut_ref[pair, c]
+        window = sent[pair, c]
         fill = jnp.zeros((cap - HALO, columns), F32)
         above = jnp.concatenate([edge_above[c, 8 - HALO : 8, :], fill], 0)
         first = (row < HALO) & (pair == 0) & (band > 0)
@@ -177,17 +185,29 @@
             window = jnp.where(last, below, window)
         return window
 
-    def cut(c, _):
-        for r in list(range(chips - 1, -1, -1)):
-            if r:
+    def cut(c, first):
+        for r in range(chips - 1, -1, -1):
+            @pl.when(jnp.logical_not(inner[r]))
+            def _(r=r):
                 sent[at(r), c] = rimmed(at(r), c)
-                outgoing(r, c).start()
-            else:
-                own[chip, c] = rimmed(chip, c)
+                if r:
+                    outgoing(r, c).start()
+
+            if r and not first:
+                @pl.when(inner[r])
+                def _(r=r):
+                    outgoing(r, c).start()
+
+            if r == 0:
+                own[chip, c] = sent[chip, c]
                 passing(0, c).start()
-        return 0
-
-    lax.fori_loop(0, share, cut, 0)
+
+    cut(0, True)
+    if share > 1:
+        @pl.loop(1, share)
+        def _(c):
+            cut(c, False)
+
     for c in range(share):
         dual_load(c).start()
     lax.fori_loop(0, low_ref.shape[0], build, 0)
@@ -267,7 +287,7 @@
                 return 0
 
             lax.fori_loop(0, kinds, one_kind, 0)
-            for target, half in ((own, core), (other, 1 - core)):
+            for target, half in ((other, 1 - core), (own, core)):
                 def place(j, _, target=target, half=half):
                     loaded = [terms[step, 2 * j + half] for step in range(kinds)]
                     merged = jnp.zeros((span, columns), F32)
@@ -283,8 +303,9 @@
                     return 0
 
                 lax.fori_loop(0, GROUP // 2, place, 0)
-        for r in list(range(chips - 1, -1, -1)):
-            homing(r, c).start()
+                if target is other and g == devices // GROUP - 1:
+                    for r in range(chips - 1, -1, -1):
+                        homing(r, c).start()
         next_store(c).start()
         for r in list(range(chips - 1, -1, -1)):
             homing(r, c).wait_recv()
@@ -339,7 +360,7 @@
             jax.ShapeDtypeStruct(dual.shape, dual.dtype), jax.ShapeDtypeStruct(windows, F32),
             rim, rim,
         ),
-        in_specs=[smem, smem, smem, vmem, free, free],
+        in_specs=[smem, smem, smem, free, free, free],
         out_specs=(free, vmem, vmem, vmem),
         scratch_shapes=[
             *[pltpu.VMEM(windows, F32)] * 4,
@@ -351,7 +372,7 @@
             pltpu.VMEM((kinds // 2, 2 * columns, 2 * columns), BF16),
             pltpu.VMEM((kinds // 2, 2 * columns, columns), BF16),
             *[pltpu.VMEM((share, 8, columns), F32)] * 3,
-            dma((share,)), dma((share,)), dma((4,)), dma((4,)),
+            dma, dma((share,)), dma((share,)), dma((4,)), dma((4,)),
             *[dma((chips, share))] * 8,
         ],
         compiler_params=pltpu.CompilerParams(
@@ -394,8 +415,8 @@
 
 
 def join_kernel(
-    cap, rows_ref, windows_ref, above_ref, below_ref, made_ref, out_ref, next_ref,
-    padded, staged, load_sems, store_sems,
+    cap, rows_ref, windows_hbm, above_hbm, below_hbm, made_ref, out_ref, next_ref,
+    padded, staged, windows_ref, above_ref, below_ref, load_sems, store_sems, part_sems,
 ):
     rows = out_ref.shape[1]
     subbands = made_ref.shape[0]
@@ -407,12 +428,20 @@
         pltpu.make_async_copy(staged.at[s], next_ref.at[s], store_sems.at[s])
         for s in range(subbands)
     ]
-    for load in loads:
-        load.start()
+    parts = [
+        pltpu.make_async_copy(source, target, part_sems.at[i])
+        for i, (source, target) in enumerate(
+            [(windows_hbm, windows_ref), (above_hbm, above_ref), (below_hbm, below_ref)]
+        )
+    ]
+    for copy in parts + loads:
+        copy.start()
     padded[...] = jnp.zeros_like(padded)
     starts = facet_starts(rows_ref)
     band, bands = lax.axis_index("grp"), lax.axis_size("grp")
 
+    for copy in parts:
+        copy.wait()
     for pair in range(windows_ref.shape[0]):
         begin = starts[2 * pair] + (LEAD - HALO)
         base = pl.multiple_of((begin // 8) * 8, 8)
@@ -448,15 +477,19 @@
             jax.ShapeDtypeStruct((channels, rows, columns), F32),
             jax.ShapeDtypeStruct(made.shape, made.dtype),
         ),
-        in_specs=[pl.BlockSpec(memory_space=pltpu.SMEM), vmem, vmem, vmem, free],
+        in_specs=[pl.BlockSpec(memory_space=pltpu.SMEM), free, free, free, free],
         out_specs=(vmem, free),
         scratch_shapes=[
             pltpu.VMEM((channels, LEAD + rows + cap + 16, columns), F32),
             pltpu.VMEM(made.shape, made.dtype),
+            pltpu.VMEM(windows.shape, F32),
+            pltpu.VMEM(above.shape, F32),
+            pltpu.VMEM(below.shape, F32),
             pltpu.SemaphoreType.DMA((made.shape[0],)),
             pltpu.SemaphoreType.DMA((made.shape[0],)),
+            pltpu.SemaphoreType.DMA((3,)),
         ],
-        compiler_params=pltpu.CompilerParams(vmem_limit_bytes=48 * 2**20),
+        compiler_params=pltpu.CompilerParams(vmem_limit_bytes=60 * 2**20),
     )(facet_rows, windows, above, below, made)
 
 

time: 119 us -> 112 us (0.941)
  Pallas kernels: 109 us -> 105 us
  local copies, waits for them, and re-layouts: 4.92 us -> 1.95 us
    pallas_call x1, Pallas kernels: 97.6 us -> 93.6 us  [whole(): pl.pallas_call(functools.partial(whole_kernel, cap), out_shape=(jax.Shape...]
    cond x14 -> x8, local copies, waits for them, and re-layouts: 4.16 us -> 1.2 us
where the time goes in v5:
time: 112 us; the launch traced here: 110 us
  Pallas kernels  105 us (94%)
  local copies, waits for them, and re-layouts  1.95 us (2%)
  between operations  1.47 us (1%)
  other arithmetic  1.41 us (1%)
    pallas_call x1, Pallas kernels, whole(): pl.pallas_call(functools.partial(whole_kernel, cap), out_shape=(jax.Shape...  93.6 us
    pallas_call x1, Pallas kernels, join(): pl.pallas_call(functools.partial(join_kernel, cap), out_shape=(jax.ShapeD...  9.27 us

profile of v5, /device:TPU:4, one launch (start us, length us, event | category | flops | bytes accessed | tf_op | source)
XLA Modules:
  0.0 110.1 jit_solution(12683155932791577225)
XLA Ops:
  0.6 0.7 convert_element_type.11
  1.3 0.8 reshape.19
  2.0 0.1 reduce_sum.9
  2.2 0.6 reduce_max.9
  3.5 106.5 %conditional.1 = (f32[4,384,256]{2,1,0:T(8,128)}, bf16[8,32,72,256]{3,2,1,0:T(8,128)(2,1)}) conditional(s32[]{:T(128)} %clamp.3, (s32[4,8]{1,0:T(4,128)}, f32[4,384,256]{2,1,0:T(8,128)}, f32[2,4]{1,0:T(2,128)S(1)}, f32[8]{0:T(128)}, bf16[8,32,72,256]{3,2,1,0:T(8,128)(2,1)}) %tuple.19, (s32[4,8]{1,0:T(4,128)}, ...), branch_computations={%region_2.0_spmd, %region_3.0_spmd, %region_4.0_spmd} | conditional | bytes 16253696 | solution.py:519
  3.5 0.0 copy-start.3
  3.5 0.0 copy-start.6
  3.5 0.0 copy-start.9
  3.5 2.1 %branch_0_fun.3.cut_ref = f32[4,4,104,256]{3,2,1,0:T(8,128)S(1)} custom-call(s32[4,8]{1,0:T(4,128)} %get-tuple-element.30.rows_ref, f32[4,384,256]{2,1,0:T(8,128)} %get-tuple-element.75.image_ref), custom_call_target="tpu_custom_call" | custom-call | tf_op jit(solution)/shard_map/cond/branch_0_fun/pallas_call | solution.py:407
  5.6 0.0 copy-start.2
  5.7 1.2 %copy-done.2 = f32[4,4,104,256]{3,2,1,0:T(8,128)} copy-done((f32[4,4,104,256]{3,2,1,0:T(8,128)}, f32[4,4,104,256]{3,2,1,0:T(8,128)S(1)}, u32[]{:S(2)}) %copy-start.2) | copy-done | bytes 1703960 | tf_op jit(solution)/shard_map/cond
  6.8 0.0 copy-done.3
  6.8 0.0 copy-done.6
  6.8 0.0 copy-done.9
  6.8 93.6 %branch_0_fun.4 = (bf16[8,8,4,72,256]{4,3,2,1,0:T(8,128)(2,1)}, f32[4,4,104,256]{3,2,1,0:T(8,128)}, f32[4,8,256]{2,1,0:T(8,128)}, f32[4,8,256]{2,1,0:T(8,128)}) custom-call(s32[4,8]{1,0:T(4,128)S(1)} %copy-done.6, f32[2,4]{1,0:T(2,128)S(1)} %get-tuple-element.31.low_ref, f32[8]{0:T(128)S(1)} %copy-done.9, f32[4,4,104,256]{3,2,1,0:T(8,128)} %copy-done.2, ...), custom_call_target="tpu_custom_call" | custom-call | tf_op jit(solution)/shard_map/cond/branch_0_fun/pallas_call | solution.py:357
  100.4 9.3 %branch_0_fun.5 = (f32[4,384,256]{2,1,0:T(8,128)}, bf16[8,8,4,72,256]{4,3,2,1,0:T(8,128)(2,1)}) custom-call(s32[4,8]{1,0:T(4,128)S(1)} %copy-done.6, f32[4,4,104,256]{3,2,1,0:T(8,128)} %get-tuple-element.35.windows_hbm, f32[4,8,256]{2,1,0:T(8,128)} %get-tuple-element.36.above_hbm, f32[4,8,256]{2,1,0:T(8,128)} %get-tuple-element.37.below_hbm, ...), custom_call_target="tpu_custom_call" | custom-call | tf_op jit(solution)/shard_map/cond/branch_0_fun/pallas_call | solution.py:474
Async XLA Ops:
  3.5 3.4 %copy-start.3 = (f32[4,384,256]{2,1,0:T(8,128)S(1)}, f32[4,384,256]{2,1,0:T(8,128)}, u32[]{:S(2)}) copy-start(f32[4,384,256]{2,1,0:T(8,128)} %get-tuple-element.75.image_ref) | copy-start | bytes 4718596 | tf_op jit(solution)/shard_map/cond
  3.5 3.4 %copy-start.6 = (s32[4,8]{1,0:T(4,128)S(1)}, s32[4,8]{1,0:T(4,128)}, u32[]{:S(2)}) copy-start(s32[4,8]{1,0:T(4,128)} %get-tuple-element.30.rows_ref) | copy-start | bytes 388 | tf_op jit(solution)/shard_map/cond
  3.5 3.3 %copy-start.9 = (f32[8]{0:T(128)S(1)}, f32[8]{0:T(128)}, u32[]{:S(2)}) copy-start(f32[8]{0:T(128)} %get-tuple-element.78.thresholds_ref) | copy-start | bytes 100 | tf_op jit(solution)/shard_map/cond
  5.6 1.2 %copy-start.2 = (f32[4,4,104,256]{3,2,1,0:T(8,128)}, f32[4,4,104,256]{3,2,1,0:T(8,128)S(1)}, u32[]{:S(2)}) copy-start(f32[4,4,104,256]{3,2,1,0:T(8,128)S(1)} %branch_0_fun.3.cut_ref) | copy-start | bytes 5111812 | tf_op jit(solution)/shard_map/cond
